TPU v7x, 32 devices: a whole 2x2x4 slice. The times are simulated.
32 devices in a mesh: scen: 1, grp: 16 (over z, y, core), pen: 2 (over x).
Axes of the slice: x: 2, y: 2, z: 4, core: 2. Of those that a mesh axis runs over, the one named last changes fastest.
Arguments:
- prec_state: float32 [1, 128, 128, 128], P('scen', 'grp', 'pen'), may hold values from -6 to 6
- farm_state: float32 [1, 128, 128, 256], P('scen', 'grp', 'pen'), may hold values from -6 to 6
- yaw_angles: float32 [2, 64], replicated, may hold values from -0.6 to 0.6
- plane_source: int32 [16], replicated, may hold values from 0 to 127, as said below
- cell_index: int32 [16, 2, 128], P('grp', 'pen'), may hold values from 0 to 131071, as said below
- cell_turbine: int32 [16, 2, 128], P('grp', 'pen'), may hold values from 0 to 63
Outputs:
- prec_final: float32 [1, 128, 128, 128], P('scen', 'grp', 'pen')
- farm_final: float32 [1, 128, 128, 256], P('scen', 'grp', 'pen')
- sensitivity: float32 [1, 128, 128, 256], P('scen', 'grp', 'pen')
- yaw_grad: float32 [2, 64], replicated
Inputs may be any that keep to these rules, and one draw needn't show every extreme that they name: `plane_source`: 16 distinct planes; plane 0 and plane 128 - 1 are always among them. `cell_index`: distinct within each farm device; index (row * 64 + z) * 256 + x of that device's block.
All inputs are finite; a program needn't handle non-finite values.
Results may differ from a plain program's by a relative error of at most 0.00012.
Values sent between devices are 32-bit elements; how exact they have to be, the bound alone decides.
A program may use at most 64 MiB of HBM per device.

v0:
```python
import functools

import jax
import jax.numpy as jnp
from jax import lax
from jax.experimental import pallas as pl
from jax.experimental.pallas import tpu as pltpu
from jax.sharding import PartitionSpec as P

NF = 16
TURB = 64
COURANT = 0.3
VISC_BASE = 0.03
VISC_SLOPE = 0.03
SLOPE_EPS = 0.01
FORCE_GAIN = 0.3
POWER_GAIN = 0.002

MESH = pl.DeviceIdType.MESH
VMEM = pl.BlockSpec(memory_space=pltpu.VMEM)
HBM = pl.BlockSpec(memory_space=pltpu.HBM)
SMEM = pl.BlockSpec(memory_space=pltpu.SMEM)
F32 = jnp.float32
BF16 = jnp.bfloat16


def split3(b):
    high = b.astype(BF16)
    rest = b - high.astype(F32)
    mid = rest.astype(BF16)
    low = (rest - mid.astype(F32)).astype(BF16)
    return high, mid, low


def dot(a, b):
    return jnp.dot(a, b, preferred_element_type=F32)


def advance_plane(centre, upper_a, lower_a, upper_z, lower_z, upper_l, lower_l, lower_x):
    slope_a = 0.5 * (upper_a - lower_a)
    slope_l = 0.5 * (upper_l - lower_l)
    slope_z = 0.5 * (upper_z - lower_z)
    viscosity = VISC_BASE + VISC_SLOPE * jnp.sqrt(
        slope_a * slope_a + slope_l * slope_l + slope_z * slope_z + SLOPE_EPS
    )
    laplacian = upper_a + lower_a + upper_l + lower_l + upper_z + lower_z - 6.0 * centre
    return centre - COURANT * (centre - lower_x) + viscosity * laplacian


def periodic_row(src, i, lead_is_x):
    centre = src[i]
    depth, lanes = centre.shape
    upper_l = pltpu.roll(centre, lanes - 1, 1)
    lower_l = pltpu.roll(centre, 1, 1)
    upper_z = pltpu.roll(centre, depth - 1, 0)
    lower_z = pltpu.roll(centre, 1, 0)
    upper_a = src[i + 1]
    lower_a = src[i - 1]
    lower_x = lower_a if lead_is_x else lower_l
    return advance_plane(centre, upper_a, lower_a, upper_z, lower_z, upper_l, lower_l, lower_x)


def farm_kernel(
    sizes, v_in, u_in, index_in, turbine_in, yaw_in, ps_ref,
    prec_ref, farm_ref, sens_ref, grad_ref,
    fp_ref, vp_ref, w_ref, cb_ref,
    v_ref, u_ref, cell_ref, index_ref, turbine_ref, yaw_ref, in_sem,
    vedge, uedge, bsend, rbody, wedge,
    v1, vw1, vw2, c0, c1, w0, w1, u1, u2, lam, nu, ry, rz, am, bm, gc0, gc1, total_a, total_b,
    near_send, near_recv, far_send, far_recv, edge_send, edge_recv, a_send, a_recv, b_send, b_recv,
):
    g = lax.axis_index("grp")
    p = lax.axis_index("pen")
    q = 1 - p
    ns, n, m = sizes
    up = lax.rem(g + 1, n)
    down = lax.rem(g + n - 1, n)
    planes, zd, fy = v_ref.shape
    rows, _, fx = u_ref.shape
    depth = zd + 8
    px = w_ref.shape[2]
    scen = lax.axis_index("scen")
    low = lax.rem(g, 4)
    high = g // 4
    upper = n // 4

    barrier = pltpu.get_barrier_semaphore()

    def greet(d, carry):
        pl.semaphore_signal(
            barrier, inc=1, device_id={"grp": lax.rem(g + d, n), "pen": p}, device_id_type=MESH
        )
        return carry

    lax.fori_loop(1, n, greet, 0)
    for target in (up, down) + tuple(high * 4 + k for k in range(4)):
        pl.semaphore_signal(barrier, inc=1, device_id={"grp": target, "pen": q}, device_id_type=MESH)

    def line(d):
        other = lax.rem(scen * upper + high + d, ns * upper)
        return {"scen": other // upper, "grp": lax.rem(other, upper) * 4 + low, "pen": p}

    def greet_line(d, carry):
        pl.semaphore_signal(barrier, inc=1, device_id=line(d), device_id_type=MESH)
        return carry

    lax.fori_loop(1, ns * upper, greet_line, 0)

    loads = [
        pltpu.make_async_copy(src, dst, in_sem.at[i])
        for i, (src, dst) in enumerate((
            (v_in, v_ref), (index_in, index_ref), (turbine_in, turbine_ref), (u_in, u_ref), (yaw_in, yaw_ref),
        ))
    ]
    for load in loads:
        load.start()
    loads[0].wait()

    vedge[:, 0:4] = v_ref[:, 0:4]
    vedge[:, 4:8] = v_ref[:, zd - 4 : zd]
    for x in range(planes):
        plane = v_ref[x]
        both = jnp.concatenate(
            [pltpu.roll(plane, 4, 1), pltpu.roll(plane, fy - 4, 1)], axis=0
        )
        bsend[:, x, :] = both.T

    for load in loads[1:]:
        load.wait()
    uedge[:, 0:4] = u_ref[:, 0:4]
    uedge[:, 4:8] = u_ref[:, zd - 4 : zd]
    cell_ref[...] = jnp.zeros_like(cell_ref)
    cell_ref[0:1] = index_ref[...]
    cell_ref[1:2] = turbine_ref[...]

    pl.semaphore_wait(barrier, (n - 1) + 6 + (ns * upper - 1))

    def far(d):
        target = lax.rem(g + d, n)
        return pltpu.make_async_remote_copy(
            src_ref=bsend.at[pl.ds(target * 8, 8)],
            dst_ref=rbody.at[:, pl.ds(g * planes, planes)],
            send_sem=far_send.at[d],
            recv_sem=far_recv.at[d],
            device_id={"grp": target, "pen": p},
            device_id_type=MESH,
        )

    def far_start(d, carry):
        far(d).start()
        return carry


    moves = [
        (u_ref.at[rows - 4 : rows], fp_ref.at[0:4, 0:zd], up, p),
        (u_ref.at[0:4], fp_ref.at[rows + 4 : rows + 8, 0:zd], down, p),
        (uedge, fp_ref.at[4 : rows + 4, zd : zd + 8], g, q),
        (uedge.at[rows - 4 : rows], fp_ref.at[0:4, zd : zd + 8], up, q),
        (uedge.at[0:4], fp_ref.at[rows + 4 : rows + 8, zd : zd + 8], down, q),
        (v_ref.at[planes - 2 : planes], vp_ref.at[0:2, 0:zd], up, p),
        (v_ref.at[0:2], vp_ref.at[planes + 2 : planes + 4, 0:zd], down, p),
        (vedge, vp_ref.at[2 : planes + 2, zd : zd + 8], g, q),
        (vedge.at[planes - 2 : planes], vp_ref.at[0:2, zd : zd + 8], up, q),
        (vedge.at[0:2], vp_ref.at[planes + 2 : planes + 4, zd : zd + 8], down, q),
        (cell_ref, cb_ref.at[1], up, p),
        (cell_ref, cb_ref.at[2], down, p),
        (cell_ref, cb_ref.at[3], g, q),
        (cell_ref, cb_ref.at[4], up, q),
        (cell_ref, cb_ref.at[5], down, q),
    ]
    copies = [
        pltpu.make_async_remote_copy(
            src_ref=src, dst_ref=dst, send_sem=near_send.at[i], recv_sem=near_recv.at[i],
            device_id={"grp": tg, "pen": tp}, device_id_type=MESH,
        )
        for i, (src, dst, tg, tp) in enumerate(moves)
    ]
    upward, downward, aside = (0, 3), (1, 4), (2,)
    for i in range(10, 15):
        copies[i].start()
    lax.fori_loop(1, n, far_start, 0)
    for i in range(5, 10):
        copies[i].start()
    for i in aside:
        copies[i].start()

    @pl.when(g < n - 1)
    def _():
        for i in upward:
            copies[i].start()

    @pl.when(g > 0)
    def _():
        for i in downward:
            copies[i].start()

    fp_ref[4 : rows + 4, 0:zd] = u_ref[...]
    vp_ref[2 : planes + 2, 0:zd] = v_ref[...]
    cb_ref[0] = cell_ref[...]
    rbody[:, pl.ds(g * planes, planes)] = bsend[pl.ds(g * 8, 8)]

    for i in range(10, 15):
        copies[i].wait()

    lane128 = lax.broadcasted_iota(jnp.int32, (1, 128), 1)
    wanted = jnp.full((1, 128), -1, jnp.int32)
    for j in range(NF):
        wanted = jnp.where(lane128 == j, ps_ref[j], wanted)
    pick = (lax.broadcasted_iota(jnp.int32, (px, 128), 0) == wanted).astype(BF16)

    def inlet(row):
        hi, mid, lo = split3(row)
        return (dot(lo, pick) + dot(mid, pick)) + dot(hi, pick)

    cosine = jnp.cos(yaw_ref[...])
    sine = jnp.sin(yaw_ref[...])
    index = [cb_ref[k, 0:1, :] for k in range(6)]
    turned = [cb_ref[k].T for k in range(6)]
    count = index[0].shape[1]
    lane_t = lax.broadcasted_iota(jnp.int32, (count, TURB), 1)

    def at_turbine(k, table):
        return jnp.sum(jnp.where(turned[k][:, 1:2] == lane_t, table, 0.0), axis=1, keepdims=True)

    lane_x = lax.broadcasted_iota(jnp.int32, (count, fx), 1)
    sub_z = lax.broadcasted_iota(jnp.int32, (depth, count), 0)
    along = [lax.rem(turned[k][:, 0:1], fx) for k in range(6)]

    def spread(k, s):
        return jnp.where(along[k] == lane_x, at_turbine(k, cosine[s : s + 1]), 0.0)

    sub_column = lax.broadcasted_iota(jnp.int32, (depth, 1), 0)
    z_global = jnp.where(
        sub_column < zd + 4, p * zd + sub_column, p * zd + sub_column - depth
    )
    z_ok = (z_global >= 0) & (z_global < lax.axis_size("pen") * zd)

    def row_ok(r):
        y = g * rows + (r - 4)
        return z_ok & (y >= 0) & (y < n * rows)

    for body, edge, first, last, offset in (
        (1, 4, 0, 4, rows - 4),
        (0, 3, 4, rows + 4, -4),
        (2, 5, rows + 4, rows + 8, -(rows + 4)),
    ):
        values = [
            split3(jnp.concatenate([spread(body, s), spread(edge, s)], axis=0)) for s in range(2)
        ]
        z_body = lax.rem(index[body] // fx, zd)
        y_body = index[body] // (fx * zd)
        z_edge = lax.rem(index[edge] // fx, zd)
        y_edge = index[edge] // (fx * zd)
        z_edge = jnp.where(z_edge < 4, z_edge + zd, jnp.where(z_edge >= zd - 4, z_edge + 8, -1))
        for r in range(first, last):
            yl = r + offset
            hot_body = (sub_z == z_body) & (y_body == yl)
            hot_edge = (sub_z == z_edge) & (y_edge == yl)
            hot = jnp.concatenate([hot_body.astype(F32), hot_edge.astype(F32)], axis=1).astype(BF16)
            for s, field in ((0, c0), (1, c1)):
                hi, mid, lo = values[s]
                total = (dot(hot, lo) + dot(hot, mid)) + dot(hot, hi)
                field[r] = jnp.where(row_ok(r), total, 0.0)

    def far_wait(d, carry):
        far(d).wait()
        return carry

    lax.fori_loop(1, n, far_wait, 0)

    for i in range(8):
        flipped = rbody[i].T
        for h in range(2):
            part = flipped[h * zd : (h + 1) * zd]
            w_ref[h * 8 + i, 0:zd] = part
            wedge[h * 8 + i, 0:4] = part[0:4]
            wedge[h * 8 + i, 4:8] = part[zd - 4 : zd]
    last = pltpu.make_async_remote_copy(
        src_ref=wedge, dst_ref=w_ref.at[:, zd : zd + 8], send_sem=edge_send, recv_sem=edge_recv,
        device_id={"grp": g, "pen": q}, device_id_type=MESH,
    )
    last.start()

    for i in range(5, 10):
        copies[i].wait()

    for i in range(1, planes + 3):
        v1[i] = periodic_row(vp_ref, i, True)
    for i in range(2, planes + 2):
        prec_ref[i - 2] = periodic_row(v1, i, True)[0:zd]

    for i in aside:
        copies[i].wait()

    @pl.when(g < n - 1)
    def _():
        for i in upward:
            copies[i].wait_send()
        for i in downward:
            copies[i].wait_recv()

    @pl.when(g > 0)
    def _():
        for i in downward:
            copies[i].wait_send()
        for i in upward:
            copies[i].wait_recv()

    last.wait()


    for i in range(1, 15):
        vw1[i] = periodic_row(w_ref, i, False)
    for i in range(2, 14):
        vw2[i] = periodic_row(vw1, i, False)

    lane_f = lax.broadcasted_iota(jnp.int32, (depth, fx), 1)
    in_fringe = lane_f < NF
    blank = jnp.zeros((depth, fx - 128), F32)

    def fringed(planes_in, field):
        wide = jnp.concatenate([inlet(planes_in), blank], axis=1)
        return jnp.where(in_fringe, wide, field)

    for r in range(16):
        field = fringed(vw1[r], fp_ref[r]) if 1 <= r < 15 else jnp.where(in_fringe, 0.0, fp_ref[r])
        w0[r] = jnp.where(row_ok(r), field, 0.0)

    def forward(step, src, r, cos_field):
        field = src[r]
        upper_y = src[r + 1]
        lower_y = src[r - 1]
        upper_z = pltpu.roll(field, depth - 1, 0)
        lower_z = pltpu.roll(field, 1, 0)
        behind = jnp.where(lane_f == 0, field, pltpu.roll(field, 1, 1))
        slope_y = 0.5 * (upper_y - lower_y)
        slope_z = 0.5 * (upper_z - lower_z)
        square = slope_y * slope_y + slope_z * slope_z + SLOPE_EPS
        inverse = lax.rsqrt(square)
        viscosity = VISC_BASE + VISC_SLOPE * (square * inverse)
        laplacian = upper_y + lower_y + upper_z + lower_z - 4.0 * field
        moved = field - COURANT * (field - behind) + viscosity * laplacian
        c = cos_field[r]
        share = (0.5 * VISC_SLOPE) * laplacian * inverse
        nu[step, r] = viscosity
        ry[step, r] = share * slope_y
        rz[step, r] = share * slope_z
        return moved - FORCE_GAIN * (c * c) * field

    for r in range(1, 15):
        new = forward(0, w0, r, c0)
        u1[r] = new
        field = fringed(vw2[r], new) if 2 <= r < 14 else jnp.where(in_fringe, 0.0, new)
        w1[r] = jnp.where(row_ok(r), field, 0.0)
    for r in range(2, 14):
        new = forward(1, w1, r, c1)
        u2[r] = new
        c = c1[r]
        lam[r] = (2.0 * POWER_GAIN) * (c * c * c) * new
    for r in range(4, rows + 4):
        farm_ref[r - 4] = u2[r][0:zd]
        c = c1[r]
        term = c * (2.0 * FORCE_GAIN * w1[r] * lam[r] - 3.0 * POWER_GAIN * c * u2[r] * u2[r])
        gc1[r - 4] = term[0:zd]

    def spread_terms(step, r):
        value = lam[r]
        am[r] = value * nu[step, r]
        bm[r] = value * ry[step, r]

    def backward(step, r, cos_field):
        value = lam[r]
        a = am[r]
        b = value * rz[step, r]
        c = cos_field[r]
        ahead = jnp.where(lane_f == fx - 1, 0.0, pltpu.roll(value, fx - 1, 1))
        total = value * ((1.0 - COURANT) - FORCE_GAIN * (c * c)) + COURANT * ahead - 4.0 * a
        total = total + (am[r - 1] + bm[r - 1]) + (am[r + 1] - bm[r + 1])
        total = total + pltpu.roll(a + b, 1, 0) + pltpu.roll(a - b, depth - 1, 0)
        return jnp.where(in_fringe, 0.0, total)

    for r in range(2, 14):
        spread_terms(1, r)
    for r in range(3, 13):
        c = c0[r]
        value = backward(1, r, c1) + (2.0 * POWER_GAIN) * (c * c * c) * u1[r]
        u2[r] = jnp.where(row_ok(r), value, 0.0)
    for r in range(3, 13):
        lam[r] = u2[r]
    for r in range(4, rows + 4):
        c = c0[r]
        term = c * (2.0 * FORCE_GAIN * w0[r] * lam[r] - 3.0 * POWER_GAIN * c * u1[r] * u1[r])
        gc0[r - 4] = term[0:zd]
    for r in range(3, 13):
        spread_terms(0, r)
    for r in range(4, rows + 4):
        sens_ref[r - 4] = backward(0, r, c0)[0:zd]

    flat = turned[0][:, 0:1] // fx
    take = (flat == lax.broadcasted_iota(jnp.int32, (count, rows * zd), 1)).astype(F32).astype(BF16)
    total_a[low * m + p] = jnp.zeros(total_a.shape[1:], F32)
    mine = total_a.at[low * m + p]
    for s, terms in ((0, gc0), (1, gc1)):
        hi, mid, lo = split3(terms[...].reshape(rows * zd, fx))
        lines = (dot(take, lo) + dot(take, mid)) + dot(take, hi)
        value = jnp.sum(jnp.where(along[0] == lane_x, lines, 0.0), axis=1, keepdims=True)
        value = value * at_turbine(0, sine[s : s + 1])
        mine[s : s + 1, 0:TURB] = jnp.sum(
            jnp.where(turned[0][:, 1:2] == lane_t, value, 0.0), axis=0, keepdims=True
        )

    def near_copy(d):
        other = lax.rem(low * m + p + d, 4 * m)
        return pltpu.make_async_remote_copy(
            src_ref=total_a.at[low * m + p], dst_ref=total_a.at[low * m + p],
            send_sem=a_send.at[d], recv_sem=a_recv.at[d],
            device_id={"grp": high * 4 + other // m, "pen": lax.rem(other, m)}, device_id_type=MESH,
        )

    def line_copy(d):
        return pltpu.make_async_remote_copy(
            src_ref=total_b.at[scen * upper + high], dst_ref=total_b.at[scen * upper + high],
            send_sem=b_send.at[d], recv_sem=b_recv.at[d], device_id=line(d), device_id_type=MESH,
        )

    def run(make, count):
        def start(d, carry):
            make(d).start()
            return carry

        def wait(d, carry):
            make(d).wait()
            return carry

        lax.fori_loop(1, count, start, 0)
        lax.fori_loop(1, count, wait, 0)

    run(near_copy, 4 * m)
    total_b[scen * upper + high] = jnp.sum(total_a[...], axis=0)
    run(line_copy, ns * upper)
    grad_ref[...] = jnp.sum(total_b[...], axis=0)[0 : grad_ref.shape[0], 0 : grad_ref.shape[1]]


def farm_steps(sizes, v, u, index, turbine, yaw, ps):
    planes, zd, fy = v.shape
    rows, _, fx = u.shape
    ns, n, m = sizes
    px = n * planes
    depth = zd + 8
    farm = pltpu.VMEM((16, depth, fx), F32)
    dma = pltpu.SemaphoreType.DMA
    return pl.pallas_call(
        functools.partial(farm_kernel, sizes),
        out_shape=(
            jax.ShapeDtypeStruct(v.shape, F32),
            jax.ShapeDtypeStruct(u.shape, F32),
            jax.ShapeDtypeStruct(u.shape, F32),
            jax.ShapeDtypeStruct(yaw.shape, F32),
        ),
        in_specs=[HBM] * 5 + [SMEM],
        out_specs=(VMEM,) * 4,
        scratch_shapes=[
            farm,
            pltpu.VMEM((planes + 4, depth, fy), F32),
            pltpu.VMEM((16, depth, px), F32),
            pltpu.VMEM((6, 8, index.shape[1]), jnp.int32),
            pltpu.VMEM(v.shape, F32),
            pltpu.VMEM(u.shape, F32),
            pltpu.VMEM((8, index.shape[1]), jnp.int32),
            pltpu.VMEM(index.shape, jnp.int32),
            pltpu.VMEM(turbine.shape, jnp.int32),
            pltpu.VMEM(yaw.shape, F32),
            dma((5,)),
            pltpu.VMEM((planes, 8, fy), F32),
            pltpu.VMEM((rows, 8, fx), F32),
            pltpu.VMEM((fy, planes, 2 * zd), F32),
            pltpu.VMEM((8, px, 2 * zd), F32),
            pltpu.VMEM((16, 8, px), F32),
            pltpu.VMEM((planes + 4, depth, fy), F32),
            pltpu.VMEM((16, depth, px), F32),
            pltpu.VMEM((16, depth, px), F32),
            farm, farm, farm, farm, farm, farm, farm,
            pltpu.VMEM((2, 16, depth, fx), F32),
            pltpu.VMEM((2, 16, depth, fx), F32),
            pltpu.VMEM((2, 16, depth, fx), F32),
            farm, farm,
            pltpu.VMEM(u.shape, F32),
            pltpu.VMEM(u.shape, F32),
            pltpu.VMEM((4 * m, 8, 128), F32),
            pltpu.VMEM((ns * n // 4, 8, 128), F32),
            dma((15,)), dma((15,)), dma((n,)), dma((n,)), dma, dma,
            dma((4 * m,)), dma((4 * m,)), dma((ns * n // 4,)), dma((ns * n // 4,)),
        ],
        compiler_params=pltpu.CompilerParams(
            collective_id=0, has_side_effects=True, vmem_limit_bytes=63 * 1024 * 1024
        ),
        name="farm_steps",
    )(v, u, index, turbine, yaw, ps)


def shards(sizes, prec_state, farm_state, yaw_angles, plane_source, cell_index, cell_turbine):
    prec, farm, sens, yaw_grad = farm_steps(
        sizes, prec_state[0], farm_state[0], cell_index[0], cell_turbine[0], yaw_angles,
        plane_source,
    )
    return (prec[None], farm[None], sens[None], yaw_grad)


def solution(mesh):
    spec = P("scen", "grp", "pen", None)
    in_specs = (spec, spec, P(), P(), P("grp", "pen", None), P("grp", "pen", None))
    out_specs = (spec, spec, spec, P())
    sizes = tuple(mesh.shape[axis] for axis in ("scen", "grp", "pen"))
    return jax.shard_map(
        functools.partial(shards, sizes), mesh=mesh, in_specs=in_specs, out_specs=out_specs,
        check_vma=False,
    )
```

profile of v0, /device:TPU:0, one launch (start us, length us, event | category | flops | bytes accessed | tf_op | source)
XLA Modules:
  0.0 44.4 jit_solution(15431945157477141653)
XLA Ops:
  0.6 39.5 %farm_steps.1 = (f32[8,64,128]{2,1,0:T(8,128)}, f32[8,64,256]{2,1,0:T(8,128)}, f32[8,64,256]{2,1,0:T(8,128)}, f32[2,64]{1,0:T(2,128)}) custom-call(f32[8,64,128]{2,1,0:T(8,128)} %bitcast.11, f32[8,64,256]{2,1,0:T(8,128)} %bitcast.7, s32[1,128]{1,0:T(1,128)} %bitcast.12, s32[1,128]{1,0:T(1,128)} %bitcast.13, f32[2,64]{1,0:T(2,128)} %yaw_in.1, s32[16]{0:T(128)} %ps_ref.1), custom_call_target="tpu_custom_call" | custom-call | tf_op jit(solution)/shard_map/farm_steps/pallas_call | solution.py:452
  40.1 0.0 copy-start.1
  40.1 1.7 %copy.14 = f32[1,8,64,128]{3,2,1,0:T(8,128)} copy(f32[1,8,64,128]{3,2,1,0:T(8,128)} %bitcast.10) | data formatting | bytes 524288
  41.8 0.0 copy-done.1
  41.8 0.0 copy-start
  41.8 0.8 %copy.15 = f32[1,8,64,256]{3,2,1,0:T(8,128)} copy(f32[1,8,64,256]{3,2,1,0:T(8,128)S(1)} %bitcast.9) | data formatting | bytes 1048576
  42.6 0.4 copy-done
  43.1 0.0 copy-start.2
  43.1 0.8 %copy.16 = f32[1,8,64,256]{3,2,1,0:T(8,128)} copy(f32[1,8,64,256]{3,2,1,0:T(8,128)S(1)} %bitcast.8) | data formatting | bytes 1048576
  43.9 0.0 copy-done.2
  43.9 0.6 %copy.17 = f32[2,64]{1,0:T(2,128)} copy(f32[2,64]{1,0:T(2,128)S(1)} %copy-done.2) | data formatting | bytes 1024
Async XLA Ops:
  40.1 1.7 %copy-start.1 = (f32[8,64,256]{2,1,0:T(8,128)S(1)}, f32[8,64,256]{2,1,0:T(8,128)}, u32[]{:S(2)}) copy-start(f32[8,64,256]{2,1,0:T(8,128)} %get-tuple-element.9) | copy-start | bytes 1572868
  41.8 1.2 %copy-start = (f32[8,64,256]{2,1,0:T(8,128)S(1)}, f32[8,64,256]{2,1,0:T(8,128)}, u32[]{:S(2)}) copy-start(f32[8,64,256]{2,1,0:T(8,128)} %get-tuple-element.10) | copy-start | bytes 1572868
  43.1 0.8 %copy-start.2 = (f32[2,64]{1,0:T(2,128)S(1)}, f32[2,64]{1,0:T(2,128)}, u32[]{:S(2)}) copy-start(f32[2,64]{1,0:T(2,128)} %get-tuple-element.19) | copy-start | bytes 1540
where the time goes:
time: 44.7 us; the launch traced here: 44.4 us
  Pallas kernels  39.5 us (88%)
  local copies, waits for them, and re-layouts  4.32 us (10%)
  between operations  0.65 us (1%)
    pallas_call x1, Pallas kernels, farm_steps(): pl.pallas_call(functools.partial(farm_kernel, sizes), out_shape=(jax.Shap...  39.5 us
    unnamed x10, local copies, waits for them, and re-layouts  4.32 us

commit v1 on v0

--- a/solution.py
+++ b/solution.py
@@ -24,12 +24,9 @@
 BF16 = jnp.bfloat16
 
 
-def split3(b):
+def split2(b):
     high = b.astype(BF16)
-    rest = b - high.astype(F32)
-    mid = rest.astype(BF16)
-    low = (rest - mid.astype(F32)).astype(BF16)
-    return high, mid, low
+    return high, (b - high.astype(F32)).astype(BF16)
 
 
 def dot(a, b):
@@ -80,31 +77,25 @@
     depth = zd + 8
     px = w_ref.shape[2]
     scen = lax.axis_index("scen")
-    low = lax.rem(g, 4)
-    high = g // 4
-    upper = n // 4
 
     barrier = pltpu.get_barrier_semaphore()
 
-    def greet(d, carry):
-        pl.semaphore_signal(
-            barrier, inc=1, device_id={"grp": lax.rem(g + d, n), "pen": p}, device_id_type=MESH
-        )
-        return carry
-
-    lax.fori_loop(1, n, greet, 0)
-    for target in (up, down) + tuple(high * 4 + k for k in range(4)):
-        pl.semaphore_signal(barrier, inc=1, device_id={"grp": target, "pen": q}, device_id_type=MESH)
+    def peer(d):
+        other = lax.rem(g * m + p + d, n * m)
+        return {"grp": other // m, "pen": lax.rem(other, m)}
 
     def line(d):
-        other = lax.rem(scen * upper + high + d, ns * upper)
-        return {"scen": other // upper, "grp": lax.rem(other, upper) * 4 + low, "pen": p}
-
-    def greet_line(d, carry):
-        pl.semaphore_signal(barrier, inc=1, device_id=line(d), device_id_type=MESH)
-        return carry
-
-    lax.fori_loop(1, ns * upper, greet_line, 0)
+        return {"scen": lax.rem(scen + d, ns), "grp": g, "pen": p}
+
+    def greet(make):
+        def run(d, carry):
+            pl.semaphore_signal(barrier, inc=1, device_id=make(d), device_id_type=MESH)
+            return carry
+
+        return run
+
+    lax.fori_loop(1, n * m, greet(peer), 0)
+    lax.fori_loop(1, ns, greet(line), 0)
 
     loads = [
         pltpu.make_async_copy(src, dst, in_sem.at[i])
@@ -133,7 +124,7 @@
     cell_ref[0:1] = index_ref[...]
     cell_ref[1:2] = turbine_ref[...]
 
-    pl.semaphore_wait(barrier, (n - 1) + 6 + (ns * upper - 1))
+    pl.semaphore_wait(barrier, (n * m - 1) + (ns - 1))
 
     def far(d):
         target = lax.rem(g + d, n)
@@ -209,8 +200,8 @@
     pick = (lax.broadcasted_iota(jnp.int32, (px, 128), 0) == wanted).astype(BF16)
 
     def inlet(row):
-        hi, mid, lo = split3(row)
-        return (dot(lo, pick) + dot(mid, pick)) + dot(hi, pick)
+        hi, lo = split2(row)
+        return dot(lo, pick) + dot(hi, pick)
 
     cosine = jnp.cos(yaw_ref[...])
     sine = jnp.sin(yaw_ref[...])
@@ -245,7 +236,7 @@
         (2, 5, rows + 4, rows + 8, -(rows + 4)),
     ):
         values = [
-            split3(jnp.concatenate([spread(body, s), spread(edge, s)], axis=0)) for s in range(2)
+            split2(jnp.concatenate([spread(body, s), spread(edge, s)], axis=0)) for s in range(2)
         ]
         z_body = lax.rem(index[body] // fx, zd)
         y_body = index[body] // (fx * zd)
@@ -258,8 +249,8 @@
             hot_edge = (sub_z == z_edge) & (y_edge == yl)
             hot = jnp.concatenate([hot_body.astype(F32), hot_edge.astype(F32)], axis=1).astype(BF16)
             for s, field in ((0, c0), (1, c1)):
-                hi, mid, lo = values[s]
-                total = (dot(hot, lo) + dot(hot, mid)) + dot(hot, hi)
+                hi, lo = values[s]
+                total = dot(hot, lo) + dot(hot, hi)
                 field[r] = jnp.where(row_ok(r), total, 0.0)
 
     def far_wait(d, carry):
@@ -391,18 +382,13 @@
         c = c0[r]
         term = c * (2.0 * FORCE_GAIN * w0[r] * lam[r] - 3.0 * POWER_GAIN * c * u1[r] * u1[r])
         gc0[r - 4] = term[0:zd]
-    for r in range(3, 13):
-        spread_terms(0, r)
-    for r in range(4, rows + 4):
-        sens_ref[r - 4] = backward(0, r, c0)[0:zd]
-
     flat = turned[0][:, 0:1] // fx
     take = (flat == lax.broadcasted_iota(jnp.int32, (count, rows * zd), 1)).astype(F32).astype(BF16)
-    total_a[low * m + p] = jnp.zeros(total_a.shape[1:], F32)
-    mine = total_a.at[low * m + p]
+    total_a[g * m + p] = jnp.zeros(total_a.shape[1:], F32)
+    mine = total_a.at[g * m + p]
     for s, terms in ((0, gc0), (1, gc1)):
-        hi, mid, lo = split3(terms[...].reshape(rows * zd, fx))
-        lines = (dot(take, lo) + dot(take, mid)) + dot(take, hi)
+        hi, lo = split2(terms[...].reshape(rows * zd, fx))
+        lines = dot(take, lo) + dot(take, hi)
         value = jnp.sum(jnp.where(along[0] == lane_x, lines, 0.0), axis=1, keepdims=True)
         value = value * at_turbine(0, sine[s : s + 1])
         mine[s : s + 1, 0:TURB] = jnp.sum(
@@ -410,34 +396,41 @@
         )
 
     def near_copy(d):
-        other = lax.rem(low * m + p + d, 4 * m)
         return pltpu.make_async_remote_copy(
-            src_ref=total_a.at[low * m + p], dst_ref=total_a.at[low * m + p],
-            send_sem=a_send.at[d], recv_sem=a_recv.at[d],
-            device_id={"grp": high * 4 + other // m, "pen": lax.rem(other, m)}, device_id_type=MESH,
+            src_ref=total_a.at[g * m + p], dst_ref=total_a.at[g * m + p],
+            send_sem=a_send.at[d], recv_sem=a_recv.at[d], device_id=peer(d), device_id_type=MESH,
         )
 
     def line_copy(d):
         return pltpu.make_async_remote_copy(
-            src_ref=total_b.at[scen * upper + high], dst_ref=total_b.at[scen * upper + high],
+            src_ref=total_b.at[scen], dst_ref=total_b.at[scen],
             send_sem=b_send.at[d], recv_sem=b_recv.at[d], device_id=line(d), device_id_type=MESH,
         )
 
-    def run(make, count):
-        def start(d, carry):
+    def start(make):
+        def run(d, carry):
             make(d).start()
             return carry
 
-        def wait(d, carry):
+        return run
+
+    def wait(make):
+        def run(d, carry):
             make(d).wait()
             return carry
 
-        lax.fori_loop(1, count, start, 0)
-        lax.fori_loop(1, count, wait, 0)
-
-    run(near_copy, 4 * m)
-    total_b[scen * upper + high] = jnp.sum(total_a[...], axis=0)
-    run(line_copy, ns * upper)
+        return run
+
+    lax.fori_loop(1, n * m, start(near_copy), 0)
+    for r in range(3, 13):
+        spread_terms(0, r)
+    for r in range(4, rows + 4):
+        sens_ref[r - 4] = backward(0, r, c0)[0:zd]
+
+    lax.fori_loop(1, n * m, wait(near_copy), 0)
+    total_b[scen] = jnp.sum(total_a[...], axis=0)
+    lax.fori_loop(1, ns, start(line_copy), 0)
+    lax.fori_loop(1, ns, wait(line_copy), 0)
     grad_ref[...] = jnp.sum(total_b[...], axis=0)[0 : grad_ref.shape[0], 0 : grad_ref.shape[1]]
 
 
@@ -452,10 +445,10 @@
     return pl.pallas_call(
         functools.partial(farm_kernel, sizes),
         out_shape=(
-            jax.ShapeDtypeStruct(v.shape, F32),
-            jax.ShapeDtypeStruct(u.shape, F32),
-            jax.ShapeDtypeStruct(u.shape, F32),
-            jax.ShapeDtypeStruct(yaw.shape, F32),
+            pltpu.VMEM(v.shape, F32),
+            pltpu.VMEM(u.shape, F32),
+            pltpu.VMEM(u.shape, F32),
+            pltpu.VMEM(yaw.shape, F32),
         ),
         in_specs=[HBM] * 5 + [SMEM],
         out_specs=(VMEM,) * 4,
@@ -486,16 +479,37 @@
             farm, farm,
             pltpu.VMEM(u.shape, F32),
             pltpu.VMEM(u.shape, F32),
-            pltpu.VMEM((4 * m, 8, 128), F32),
-            pltpu.VMEM((ns * n // 4, 8, 128), F32),
+            pltpu.VMEM((n * m, 2, 128), F32),
+            pltpu.VMEM((ns, 2, 128), F32),
             dma((15,)), dma((15,)), dma((n,)), dma((n,)), dma, dma,
-            dma((4 * m,)), dma((4 * m,)), dma((ns * n // 4,)), dma((ns * n // 4,)),
+            dma((n * m,)), dma((n * m,)), dma((ns,)), dma((ns,)),
         ],
         compiler_params=pltpu.CompilerParams(
-            collective_id=0, has_side_effects=True, vmem_limit_bytes=63 * 1024 * 1024
+            collective_id=0, has_side_effects=True, vmem_limit_bytes=56 * 1024 * 1024
         ),
         name="farm_steps",
     )(v, u, index, turbine, yaw, ps)
+
+
+def finish_kernel(*refs):
+    count = (len(refs) - 1) // 2
+    sem = refs[-1]
+    copies = [pltpu.make_async_copy(refs[i], refs[count + i], sem.at[i]) for i in range(count)]
+    for copy in copies:
+        copy.start()
+    for copy in copies:
+        copy.wait()
+
+
+def finish(*arrays):
+    return pl.pallas_call(
+        finish_kernel,
+        out_shape=tuple(jax.ShapeDtypeStruct(x.shape, F32) for x in arrays),
+        in_specs=[VMEM] * len(arrays),
+        out_specs=(HBM,) * len(arrays),
+        scratch_shapes=[pltpu.SemaphoreType.DMA((len(arrays),))],
+        name="finish",
+    )(*[pltpu.with_memory_space_constraint(x, pltpu.VMEM) for x in arrays])
 
 
 def shards(sizes, prec_state, farm_state, yaw_angles, plane_source, cell_index, cell_turbine):
@@ -503,6 +517,7 @@
         sizes, prec_state[0], farm_state[0], cell_index[0], cell_turbine[0], yaw_angles,
         plane_source,
     )
+    prec, farm, sens, yaw_grad = finish(prec, farm, sens, yaw_grad)
     return (prec[None], farm[None], sens[None], yaw_grad)
 
 

time: 44.7 us -> 39.1 us (0.87)
  local copies, waits for them, and re-layouts: 4.32 us -> 0 us
  Pallas kernels: 39.5 us -> 38.3 us
    unnamed x10 -> x0, local copies, waits for them, and re-layouts: 4.32 us -> none
    pallas_call x1 -> x2, Pallas kernels: 39.5 us -> 38.3 us  [the longest x1 37.2 us: farm_steps(): pl.pallas_call(functools.partial(farm_kernel, sizes), out_shape=(pltpu.VM...]
where the time goes in v1:
time: 39.1 us; the launch traced here: 38.9 us
  Pallas kernels  38.3 us (98%)
  between operations  0.64 us (2%)
    pallas_call x1, Pallas kernels, farm_steps(): pl.pallas_call(functools.partial(farm_kernel, sizes), out_shape=(pltpu.VM...  37.2 us
    pallas_call x1, Pallas kernels, finish(): pl.pallas_call(finish_kernel, out_shape=tuple((jax.ShapeDtypeStruct(x.sha...  1.09 us

profile of v1, /device:TPU:0, one launch (start us, length us, event | category | flops | bytes accessed | tf_op | source)
XLA Modules:
  0.0 38.9 jit_solution(11463846412721281486)
XLA Ops:
  0.6 37.2 %farm_steps.1 = (f32[8,64,128]{2,1,0:T(8,128)S(1)}, f32[8,64,256]{2,1,0:T(8,128)S(1)}, f32[8,64,256]{2,1,0:T(8,128)S(1)}, f32[2,64]{1,0:T(2,128)S(1)}) custom-call(f32[8,64,128]{2,1,0:T(8,128)} %bitcast.8, f32[8,64,256]{2,1,0:T(8,128)} %bitcast.7, s32[1,128]{1,0:T(1,128)} %bitcast.9, s32[1,128]{1,0:T(1,128)} %bitcast.10, f32[2,64]{1,0:T(2,128)} %yaw_in.1, ...), custom_call_target="tpu_custom_call" | custom-call | tf_op jit(solution)/shard_map/farm_steps/pallas_call | solution.py:445
  37.8 1.1 %finish.1 = (f32[8,64,128]{2,1,0:T(8,128)}, f32[8,64,256]{2,1,0:T(8,128)}, f32[8,64,256]{2,1,0:T(8,128)}, f32[2,64]{1,0:T(2,128)}) custom-call(f32[8,64,128]{2,1,0:T(8,128)S(1)} %get-tuple-element.12.refs_0_, f32[8,64,256]{2,1,0:T(8,128)S(1)} %get-tuple-element.13.refs_1_, f32[8,64,256]{2,1,0:T(8,128)S(1)} %get-tuple-element.14.refs_2_, ...), custom_call_target="tpu_custom_call" | custom-call | tf_op jit(solution)/shard_map/finish/pallas_call | solution.py:505

commit v2 on v1

--- a/solution.py
+++ b/solution.py
@@ -64,6 +64,7 @@
     v_ref, u_ref, cell_ref, index_ref, turbine_ref, yaw_ref, in_sem,
     vedge, uedge, bsend, rbody, wedge,
     v1, vw1, vw2, c0, c1, w0, w1, u1, u2, lam, nu, ry, rz, am, bm, gc0, gc1, total_a, total_b,
+    pick_ref, cp_ref, side_ref, part_ref,
     near_send, near_recv, far_send, far_recv, edge_send, edge_recv, a_send, a_recv, b_send, b_recv,
 ):
     g = lax.axis_index("grp")
@@ -72,6 +73,7 @@
     ns, n, m = sizes
     up = lax.rem(g + 1, n)
     down = lax.rem(g + n - 1, n)
+    odd = lax.rem(g, 2)
     planes, zd, fy = v_ref.shape
     rows, _, fx = u_ref.shape
     depth = zd + 8
@@ -84,6 +86,9 @@
         other = lax.rem(g * m + p + d, n * m)
         return {"grp": other // m, "pen": lax.rem(other, m)}
 
+    def mate(d):
+        return {"grp": lax.rem(g + d, n), "pen": p}
+
     def line(d):
         return {"scen": lax.rem(scen + d, ns), "grp": g, "pen": p}
 
@@ -94,7 +99,9 @@
 
         return run
 
-    lax.fori_loop(1, n * m, greet(peer), 0)
+    lax.fori_loop(1, n, greet(mate), 0)
+    for target in (g, up, down):
+        pl.semaphore_signal(barrier, inc=1, device_id={"grp": target, "pen": q}, device_id_type=MESH)
     lax.fori_loop(1, ns, greet(line), 0)
 
     loads = [
@@ -111,10 +118,10 @@
     vedge[:, 4:8] = v_ref[:, zd - 4 : zd]
     for x in range(planes):
         plane = v_ref[x]
-        both = jnp.concatenate(
-            [pltpu.roll(plane, 4, 1), pltpu.roll(plane, fy - 4, 1)], axis=0
-        )
-        bsend[:, x, :] = both.T
+        both = jnp.concatenate([plane, pltpu.roll(plane, fy - 6, 1)], axis=0).T
+        bsend[4 : fy + 4, x, :] = both
+        bsend[0:4, x, :] = both[fy - 4 : fy]
+        bsend[fy + 4 : fy + 8, x, :] = both[0:4]
 
     for load in loads[1:]:
         load.wait()
@@ -124,12 +131,12 @@
     cell_ref[0:1] = index_ref[...]
     cell_ref[1:2] = turbine_ref[...]
 
-    pl.semaphore_wait(barrier, (n * m - 1) + (ns - 1))
+    pl.semaphore_wait(barrier, (n - 1) + 3 + (ns - 1))
 
     def far(d):
         target = lax.rem(g + d, n)
         return pltpu.make_async_remote_copy(
-            src_ref=bsend.at[pl.ds(target * 8, 8)],
+            src_ref=bsend.at[pl.ds(target * 8 + 4 * lax.rem(target, 2), 6)],
             dst_ref=rbody.at[:, pl.ds(g * planes, planes)],
             send_sem=far_send.at[d],
             recv_sem=far_recv.at[d],
@@ -169,7 +176,6 @@
     upward, downward, aside = (0, 3), (1, 4), (2,)
     for i in range(10, 15):
         copies[i].start()
-    lax.fori_loop(1, n, far_start, 0)
     for i in range(5, 10):
         copies[i].start()
     for i in aside:
@@ -185,10 +191,12 @@
         for i in downward:
             copies[i].start()
 
+    lax.fori_loop(1, n, far_start, 0)
+
     fp_ref[4 : rows + 4, 0:zd] = u_ref[...]
     vp_ref[2 : planes + 2, 0:zd] = v_ref[...]
     cb_ref[0] = cell_ref[...]
-    rbody[:, pl.ds(g * planes, planes)] = bsend[pl.ds(g * 8, 8)]
+    rbody[:, pl.ds(g * planes, planes)] = bsend[pl.ds(g * 8 + 4 * odd, 6)]
 
     for i in range(10, 15):
         copies[i].wait()
@@ -196,12 +204,13 @@
     lane128 = lax.broadcasted_iota(jnp.int32, (1, 128), 1)
     wanted = jnp.full((1, 128), -1, jnp.int32)
     for j in range(NF):
-        wanted = jnp.where(lane128 == j, ps_ref[j], wanted)
-    pick = (lax.broadcasted_iota(jnp.int32, (px, 128), 0) == wanted).astype(BF16)
-
-    def inlet(row):
-        hi, lo = split2(row)
-        return dot(lo, pick) + dot(hi, pick)
+        wanted = jnp.where((lane128 & (NF - 1)) == j, ps_ref[j], wanted)
+    sub_x = lax.broadcasted_iota(jnp.int32, (px, 128), 0)
+    pick = jnp.concatenate(
+        [(sub_x == wanted).astype(F32), (sub_x == ps_ref[NF - 1]).astype(F32)], axis=1
+    ).astype(BF16)
+    pick_ref[0:px] = pick
+    pick_ref[px : 2 * px] = pick
 
     cosine = jnp.cos(yaw_ref[...])
     sine = jnp.sin(yaw_ref[...])
@@ -217,8 +226,10 @@
     sub_z = lax.broadcasted_iota(jnp.int32, (depth, count), 0)
     along = [lax.rem(turned[k][:, 0:1], fx) for k in range(6)]
 
+    turned_cos = [[at_turbine(k, cosine[s : s + 1]) for s in range(2)] for k in range(6)]
+
     def spread(k, s):
-        return jnp.where(along[k] == lane_x, at_turbine(k, cosine[s : s + 1]), 0.0)
+        return jnp.where(along[k] == lane_x, turned_cos[k][s], 0.0)
 
     sub_column = lax.broadcasted_iota(jnp.int32, (depth, 1), 0)
     z_global = jnp.where(
@@ -253,32 +264,45 @@
                 total = dot(hot, lo) + dot(hot, hi)
                 field[r] = jnp.where(row_ok(r), total, 0.0)
 
+    lane_r = lane128 // 8
+    lane_k = lane128 & 7
+    y_side = g * rows + lane_r - 4
+    side_ok = z_ok & (y_side >= 0) & (y_side < n * rows)
+    y_edge = g * rows + jnp.where(lane128 < 64, -1, rows)
+    edge_ok = z_ok & (y_edge >= 0) & (y_edge < n * rows)
+
+    hots, packs = [], []
+    slots = []
+    for k in range(6):
+        z_cell = lax.rem(index[k] // fx, zd)
+        if k >= 3:
+            z_cell = jnp.where(z_cell < 4, z_cell + zd, jnp.where(z_cell >= zd - 4, z_cell + 8, -1))
+        hots.append((sub_z == z_cell).astype(F32))
+        r_cell = turned[k][:, 0:1] // (fx * zd) - (-4, rows - 4, -(rows + 4))[k % 3]
+        in_front = jnp.where(along[k] < NF, (r_cell - 4) * NF + along[k], -1)
+        beside = jnp.where((along[k] >= 14) & (along[k] < 22), r_cell * 8 + along[k] - 14, -1)
+        slots.append((in_front, beside))
+        parts = []
+        for s in range(2):
+            if k % 3 == 0:
+                parts.append(jnp.where(in_front == lane128, turned_cos[k][s], 0.0))
+            else:
+                parts.append(jnp.zeros((count, 128), F32))
+            parts.append(jnp.where(beside == lane128, turned_cos[k][s], 0.0))
+        packs.append(jnp.concatenate(parts, axis=1))
+    hi, lo = split2(jnp.concatenate(packs, axis=0))
+    hot = jnp.concatenate(hots, axis=1).astype(BF16)
+    packed = dot(hot, lo) + dot(hot, hi)
+    for k in range(4):
+        part = packed[:, k * 128 : (k + 1) * 128]
+        cp_ref[k] = jnp.where(side_ok if k % 2 else z_ok, part, 0.0)
+
     def far_wait(d, carry):
         far(d).wait()
         return carry
 
-    lax.fori_loop(1, n, far_wait, 0)
-
-    for i in range(8):
-        flipped = rbody[i].T
-        for h in range(2):
-            part = flipped[h * zd : (h + 1) * zd]
-            w_ref[h * 8 + i, 0:zd] = part
-            wedge[h * 8 + i, 0:4] = part[0:4]
-            wedge[h * 8 + i, 4:8] = part[zd - 4 : zd]
-    last = pltpu.make_async_remote_copy(
-        src_ref=wedge, dst_ref=w_ref.at[:, zd : zd + 8], send_sem=edge_send, recv_sem=edge_recv,
-        device_id={"grp": g, "pen": q}, device_id_type=MESH,
-    )
-    last.start()
-
     for i in range(5, 10):
         copies[i].wait()
-
-    for i in range(1, planes + 3):
-        v1[i] = periodic_row(vp_ref, i, True)
-    for i in range(2, planes + 2):
-        prec_ref[i - 2] = periodic_row(v1, i, True)[0:zd]
 
     for i in aside:
         copies[i].wait()
@@ -297,33 +321,19 @@
         for i in upward:
             copies[i].wait_recv()
 
-    last.wait()
-
-
-    for i in range(1, 15):
-        vw1[i] = periodic_row(w_ref, i, False)
-    for i in range(2, 14):
-        vw2[i] = periodic_row(vw1, i, False)
+    side = jnp.zeros((depth, 128), F32)
+    for r in range(16):
+        side = jnp.where(lane_r == r, pltpu.roll(fp_ref[r, :, 0:128], (8 * r - 14) % 128, 1), side)
+    side_ref[...] = side
 
     lane_f = lax.broadcasted_iota(jnp.int32, (depth, fx), 1)
-    in_fringe = lane_f < NF
-    blank = jnp.zeros((depth, fx - 128), F32)
-
-    def fringed(planes_in, field):
-        wide = jnp.concatenate([inlet(planes_in), blank], axis=1)
-        return jnp.where(in_fringe, wide, field)
 
     for r in range(16):
-        field = fringed(vw1[r], fp_ref[r]) if 1 <= r < 15 else jnp.where(in_fringe, 0.0, fp_ref[r])
-        w0[r] = jnp.where(row_ok(r), field, 0.0)
-
-    def forward(step, src, r, cos_field):
-        field = src[r]
-        upper_y = src[r + 1]
-        lower_y = src[r - 1]
+        w0[r] = jnp.where(row_ok(r), fp_ref[r], 0.0)
+
+    def advance(field, upper_y, lower_y, behind, c):
         upper_z = pltpu.roll(field, depth - 1, 0)
         lower_z = pltpu.roll(field, 1, 0)
-        behind = jnp.where(lane_f == 0, field, pltpu.roll(field, 1, 1))
         slope_y = 0.5 * (upper_y - lower_y)
         slope_z = 0.5 * (upper_z - lower_z)
         square = slope_y * slope_y + slope_z * slope_z + SLOPE_EPS
@@ -331,28 +341,34 @@
         viscosity = VISC_BASE + VISC_SLOPE * (square * inverse)
         laplacian = upper_y + lower_y + upper_z + lower_z - 4.0 * field
         moved = field - COURANT * (field - behind) + viscosity * laplacian
-        c = cos_field[r]
         share = (0.5 * VISC_SLOPE) * laplacian * inverse
-        nu[step, r] = viscosity
-        ry[step, r] = share * slope_y
-        rz[step, r] = share * slope_z
-        return moved - FORCE_GAIN * (c * c) * field
+        return moved - FORCE_GAIN * (c * c) * field, viscosity, share * slope_y, share * slope_z
+
+    def forward(step, src, r, cos_field):
+        field = src[r]
+        behind = jnp.where(lane_f == 0, field, pltpu.roll(field, 1, 1))
+        new, nu[step, r], ry[step, r], rz[step, r] = advance(
+            field, src[r + 1], src[r - 1], behind, cos_field[r]
+        )
+        return new
+
+    def power_slope(c, field):
+        return (2.0 * POWER_GAIN) * (c * c * c) * field
+
+    def yaw_term(c, field, value, new):
+        return c * (2.0 * FORCE_GAIN * field * value - 3.0 * POWER_GAIN * c * new * new)
 
     for r in range(1, 15):
         new = forward(0, w0, r, c0)
         u1[r] = new
-        field = fringed(vw2[r], new) if 2 <= r < 14 else jnp.where(in_fringe, 0.0, new)
-        w1[r] = jnp.where(row_ok(r), field, 0.0)
+        w1[r] = jnp.where(row_ok(r), new, 0.0)
     for r in range(2, 14):
         new = forward(1, w1, r, c1)
         u2[r] = new
-        c = c1[r]
-        lam[r] = (2.0 * POWER_GAIN) * (c * c * c) * new
+        lam[r] = power_slope(c1[r], new)
     for r in range(4, rows + 4):
         farm_ref[r - 4] = u2[r][0:zd]
-        c = c1[r]
-        term = c * (2.0 * FORCE_GAIN * w1[r] * lam[r] - 3.0 * POWER_GAIN * c * u2[r] * u2[r])
-        gc1[r - 4] = term[0:zd]
+        gc1[r - 4] = yaw_term(c1[r], w1[r], lam[r], u2[r])[0:zd]
 
     def spread_terms(step, r):
         value = lam[r]
@@ -367,30 +383,137 @@
         ahead = jnp.where(lane_f == fx - 1, 0.0, pltpu.roll(value, fx - 1, 1))
         total = value * ((1.0 - COURANT) - FORCE_GAIN * (c * c)) + COURANT * ahead - 4.0 * a
         total = total + (am[r - 1] + bm[r - 1]) + (am[r + 1] - bm[r + 1])
-        total = total + pltpu.roll(a + b, 1, 0) + pltpu.roll(a - b, depth - 1, 0)
-        return jnp.where(in_fringe, 0.0, total)
+        return total + pltpu.roll(a + b, 1, 0) + pltpu.roll(a - b, depth - 1, 0)
 
     for r in range(2, 14):
         spread_terms(1, r)
     for r in range(3, 13):
-        c = c0[r]
-        value = backward(1, r, c1) + (2.0 * POWER_GAIN) * (c * c * c) * u1[r]
+        value = backward(1, r, c1) + power_slope(c0[r], u1[r])
         u2[r] = jnp.where(row_ok(r), value, 0.0)
     for r in range(3, 13):
         lam[r] = u2[r]
     for r in range(4, rows + 4):
-        c = c0[r]
-        term = c * (2.0 * FORCE_GAIN * w0[r] * lam[r] - 3.0 * POWER_GAIN * c * u1[r] * u1[r])
-        gc0[r - 4] = term[0:zd]
+        gc0[r - 4] = yaw_term(c0[r], w0[r], lam[r], u1[r])[0:zd]
+    for r in range(3, 13):
+        spread_terms(0, r)
+    for r in range(4, rows + 4):
+        sens_ref[r - 4] = backward(0, r, c0)[0:zd]
+
     flat = turned[0][:, 0:1] // fx
     take = (flat == lax.broadcasted_iota(jnp.int32, (count, rows * zd), 1)).astype(F32).astype(BF16)
-    total_a[g * m + p] = jnp.zeros(total_a.shape[1:], F32)
-    mine = total_a.at[g * m + p]
+    far_along = jnp.where(along[0] >= 18, along[0], -1)
     for s, terms in ((0, gc0), (1, gc1)):
         hi, lo = split2(terms[...].reshape(rows * zd, fx))
         lines = dot(take, lo) + dot(take, hi)
-        value = jnp.sum(jnp.where(along[0] == lane_x, lines, 0.0), axis=1, keepdims=True)
-        value = value * at_turbine(0, sine[s : s + 1])
+        value = jnp.where(far_along == lane_x, lines, 0.0)
+        part_ref[s] = value[:, 0:128] + value[:, 128:256]
+
+    lax.fori_loop(1, n, far_wait, 0)
+
+    base = 4 * odd
+    for i in range(6):
+        flipped = rbody[i].T
+        for h in range(2):
+            part = flipped[h * zd : (h + 1) * zd]
+            w_ref[base + h * 6 + i, 0:zd] = part
+            wedge[base + h * 6 + i, 0:4] = part[0:4]
+            wedge[base + h * 6 + i, 4:8] = part[zd - 4 : zd]
+    inner, outer = 8 - base, 12 * odd
+    mated = g + 1 - 2 * odd
+    lasts = [
+        pltpu.make_async_remote_copy(
+            src_ref=src, dst_ref=dst, send_sem=edge_send.at[i], recv_sem=edge_recv.at[i],
+            device_id={"grp": target, "pen": side_pen}, device_id_type=MESH,
+        )
+        for i, (src, dst, target, side_pen) in enumerate((
+            (wedge.at[pl.ds(base, 12)], w_ref.at[pl.ds(base, 12), zd : zd + 8], g, q),
+            (wedge.at[pl.ds(inner, 4)], w_ref.at[pl.ds(outer, 4), zd : zd + 8], mated, q),
+            (w_ref.at[pl.ds(inner, 4), 0:zd], w_ref.at[pl.ds(outer, 4), 0:zd], mated, p),
+        ))
+    ]
+    for last in lasts:
+        last.start()
+
+    for i in range(1, planes + 3):
+        v1[i] = periodic_row(vp_ref, i, True)
+    for i in range(2, planes + 2):
+        prec_ref[i - 2] = periodic_row(v1, i, True)[0:zd]
+
+    for last in lasts:
+        last.wait()
+
+    for i in range(1, 15):
+        vw1[i] = periodic_row(w_ref, i, False)
+    for i in range(2, 14):
+        vw2[i] = periodic_row(vw1, i, False)
+
+    def inlets(src, first, stop):
+        hi, lo = split2(src[first:stop].reshape((stop - first) * depth, px))
+        found = dot(jnp.concatenate([hi, lo], axis=1), pick_ref[...])
+        front = jnp.zeros((depth, 128), F32)
+        rim = front
+        beside = front
+        for r in range(first, stop):
+            part = found[(r - first) * depth : (r - first + 1) * depth]
+            if 4 <= r < 12:
+                front = jnp.where(lane128 // NF == r - 4, part[:, 0:128], front)
+            elif r == 3:
+                rim = jnp.where(lane128 < 64, part[:, 0:128], rim)
+            elif r == 12:
+                rim = jnp.where(lane128 >= 64, part[:, 0:128], rim)
+            beside = jnp.where(lane_r == r, part[:, 128:256], beside)
+        return jnp.where(z_ok, front, 0.0), jnp.where(edge_ok, rim, 0.0), beside
+
+    def front_step(field, rim, c):
+        upper_y = jnp.where(lane128 >= 112, rim, pltpu.roll(field, 112, 1))
+        lower_y = jnp.where(lane128 < 16, rim, pltpu.roll(field, 16, 1))
+        behind = jnp.where((lane128 & 15) == 0, field, pltpu.roll(field, 1, 1))
+        return advance(field, upper_y, lower_y, behind, c)[0]
+
+    def side_step(field, c):
+        return advance(field, pltpu.roll(field, 120, 1), pltpu.roll(field, 8, 1), pltpu.roll(field, 1, 1), c)
+
+    def side_back(value, c, scale, slope_y, slope_z):
+        a = value * scale
+        b = value * slope_y
+        d = value * slope_z
+        total = value * ((1.0 - COURANT) - FORCE_GAIN * (c * c)) - 4.0 * a
+        total = total + COURANT * pltpu.roll(value, 127, 1)
+        total = total + pltpu.roll(a + b, 8, 1) + pltpu.roll(a - b, 120, 1)
+        return total + pltpu.roll(a + d, 1, 0) + pltpu.roll(a - d, depth - 1, 0)
+
+    front0, rim0, beside0 = inlets(vw1, 1, 15)
+    front1, rim1, beside1 = inlets(vw2, 2, 14)
+    cf0, cs0, cf1, cs1 = (cp_ref[k] for k in range(4))
+
+    uf1 = front_step(front0, rim0, cf0)
+    uf2 = front_step(front1, rim1, cf1)
+    tf0 = yaw_term(cf0, front0, power_slope(cf0, uf1), uf1)
+    tf1 = yaw_term(cf1, front1, power_slope(cf1, uf2), uf2)
+
+    ws0 = jnp.where(side_ok, jnp.where(lane_k == 1, beside0, side_ref[...]), 0.0)
+    us1, *back0 = side_step(ws0, cs0)
+    ws1 = jnp.where(side_ok, jnp.where(lane_k == 1, beside1, us1), 0.0)
+    us2, *back1 = side_step(ws1, cs1)
+    value2 = power_slope(cs1, us2)
+    value1 = jnp.where(side_ok, side_back(value2, cs1, *back1) + power_slope(cs0, us1), 0.0)
+    ss = side_back(value1, cs0, *back0)
+    ts0 = yaw_term(cs0, ws0, value1, us1)
+    ts1 = yaw_term(cs1, ws1, value2, us2)
+
+    terms = jnp.concatenate([tf0, ts0, tf1, ts1], axis=1)[0:zd]
+    hi, lo = split2(terms)
+    z_own = lax.rem(turned[0][:, 0:1] // fx, zd)
+    take_z = (z_own == lax.broadcasted_iota(jnp.int32, (count, zd), 1)).astype(F32).astype(BF16)
+    lines = dot(take_z, lo) + dot(take_z, hi)
+    in_front = slots[0][0]
+    beside = jnp.where((along[0] >= 16) & (along[0] < 18), slots[0][1], -1)
+    total_a[g * m + p] = jnp.zeros(total_a.shape[1:], F32)
+    mine = total_a.at[g * m + p]
+    for s in range(2):
+        value = part_ref[s] + jnp.where(in_front == lane128, lines[:, s * 256 : s * 256 + 128], 0.0)
+        value = value + jnp.where(beside == lane128, lines[:, s * 256 + 128 : s * 256 + 256], 0.0)
+        value = jnp.sum(value, axis=1, keepdims=True) * at_turbine(0, sine[s : s + 1])
         mine[s : s + 1, 0:TURB] = jnp.sum(
             jnp.where(turned[0][:, 1:2] == lane_t, value, 0.0), axis=0, keepdims=True
         )
@@ -422,10 +545,18 @@
         return run
 
     lax.fori_loop(1, n * m, start(near_copy), 0)
-    for r in range(3, 13):
-        spread_terms(0, r)
-    for r in range(4, rows + 4):
-        sens_ref[r - 4] = backward(0, r, c0)[0:zd]
+
+    us2, ss, uf2 = us2[0:zd], ss[0:zd], uf2[0:zd]
+    for r in range(rows):
+        shift = (-18 - 8 * r) % 128
+        farm_ref[r, :, 0:128] = jnp.where(
+            lane128 < NF, pltpu.roll(uf2, (-NF * r) % 128, 1),
+            jnp.where(lane128 < 18, pltpu.roll(us2, shift, 1), farm_ref[r, :, 0:128]),
+        )
+        sens_ref[r, :, 0:128] = jnp.where(
+            lane128 < NF, 0.0,
+            jnp.where(lane128 < 18, pltpu.roll(ss, shift, 1), sens_ref[r, :, 0:128]),
+        )
 
     lax.fori_loop(1, n * m, wait(near_copy), 0)
     total_b[scen] = jnp.sum(total_a[...], axis=0)
@@ -466,8 +597,8 @@
             dma((5,)),
             pltpu.VMEM((planes, 8, fy), F32),
             pltpu.VMEM((rows, 8, fx), F32),
-            pltpu.VMEM((fy, planes, 2 * zd), F32),
-            pltpu.VMEM((8, px, 2 * zd), F32),
+            pltpu.VMEM((fy + 8, planes, 2 * zd), F32),
+            pltpu.VMEM((6, px, 2 * zd), F32),
             pltpu.VMEM((16, 8, px), F32),
             pltpu.VMEM((planes + 4, depth, fy), F32),
             pltpu.VMEM((16, depth, px), F32),
@@ -481,7 +612,11 @@
             pltpu.VMEM(u.shape, F32),
             pltpu.VMEM((n * m, 2, 128), F32),
             pltpu.VMEM((ns, 2, 128), F32),
-            dma((15,)), dma((15,)), dma((n,)), dma((n,)), dma, dma,
+            pltpu.VMEM((2 * px, 256), BF16),
+            pltpu.VMEM((4, depth, 128), F32),
+            pltpu.VMEM((depth, 128), F32),
+            pltpu.VMEM((2, index.shape[1], 128), F32),
+            dma((15,)), dma((15,)), dma((n,)), dma((n,)), dma((3,)), dma((3,)),
             dma((n * m,)), dma((n * m,)), dma((ns,)), dma((ns,)),
         ],
         compiler_params=pltpu.CompilerParams(

time: 39.1 us -> 37.2 us (0.951)
  Pallas kernels: 38.3 us -> 36.4 us
    pallas_call x1, Pallas kernels: 37.2 us -> 35.3 us  [farm_steps(): pl.pallas_call(functools.partial(farm_kernel, sizes), out_shape=(pltpu.VM...]
where the time goes in v2:
time: 37.2 us; the launch traced here: 37 us
  Pallas kernels  36.4 us (98%)
  between operations  0.64 us (2%)
    pallas_call x1, Pallas kernels, farm_steps(): pl.pallas_call(functools.partial(farm_kernel, sizes), out_shape=(pltpu.VM...  35.3 us
    pallas_call x1, Pallas kernels, finish(): pl.pallas_call(finish_kernel, out_shape=tuple((jax.ShapeDtypeStruct(x.sha...  1.09 us

profile of v2, /device:TPU:0, one launch (start us, length us, event | category | flops | bytes accessed | tf_op | source)
XLA Modules:
  0.0 37.0 jit_solution(3756327108048115132)
XLA Ops:
  0.6 35.3 %farm_steps.1 = (f32[8,64,128]{2,1,0:T(8,128)S(1)}, f32[8,64,256]{2,1,0:T(8,128)S(1)}, f32[8,64,256]{2,1,0:T(8,128)S(1)}, f32[2,64]{1,0:T(2,128)S(1)}) custom-call(f32[8,64,128]{2,1,0:T(8,128)} %bitcast.8, f32[8,64,256]{2,1,0:T(8,128)} %bitcast.7, s32[1,128]{1,0:T(1,128)} %bitcast.9, s32[1,128]{1,0:T(1,128)} %bitcast.10, f32[2,64]{1,0:T(2,128)} %yaw_in.1, ...), custom_call_target="tpu_custom_call" | custom-call | tf_op jit(solution)/shard_map/farm_steps/pallas_call | solution.py:576
  35.9 1.1 %finish.1 = (f32[8,64,128]{2,1,0:T(8,128)}, f32[8,64,256]{2,1,0:T(8,128)}, f32[8,64,256]{2,1,0:T(8,128)}, f32[2,64]{1,0:T(2,128)}) custom-call(f32[8,64,128]{2,1,0:T(8,128)S(1)} %get-tuple-element.12.refs_0_, f32[8,64,256]{2,1,0:T(8,128)S(1)} %get-tuple-element.13.refs_1_, f32[8,64,256]{2,1,0:T(8,128)S(1)} %get-tuple-element.14.refs_2_, ...), custom_call_target="tpu_custom_call" | custom-call | tf_op jit(solution)/shard_map/finish/pallas_call | solution.py:640

commit v3 on v2

--- a/solution.py
+++ b/solution.py
@@ -176,10 +176,9 @@
     upward, downward, aside = (0, 3), (1, 4), (2,)
     for i in range(10, 15):
         copies[i].start()
-    for i in range(5, 10):
-        copies[i].start()
     for i in aside:
         copies[i].start()
+    lax.fori_loop(1, n, far_start, 0)
 
     @pl.when(g < n - 1)
     def _():
@@ -191,7 +190,8 @@
         for i in downward:
             copies[i].start()
 
-    lax.fori_loop(1, n, far_start, 0)
+    for i in range(5, 10):
+        copies[i].start()
 
     fp_ref[4 : rows + 4, 0:zd] = u_ref[...]
     vp_ref[2 : planes + 2, 0:zd] = v_ref[...]
@@ -301,35 +301,13 @@
         far(d).wait()
         return carry
 
-    for i in range(5, 10):
-        copies[i].wait()
-
     for i in aside:
         copies[i].wait()
 
-    @pl.when(g < n - 1)
-    def _():
-        for i in upward:
-            copies[i].wait_send()
-        for i in downward:
-            copies[i].wait_recv()
-
-    @pl.when(g > 0)
-    def _():
-        for i in downward:
-            copies[i].wait_send()
-        for i in upward:
-            copies[i].wait_recv()
-
-    side = jnp.zeros((depth, 128), F32)
-    for r in range(16):
-        side = jnp.where(lane_r == r, pltpu.roll(fp_ref[r, :, 0:128], (8 * r - 14) % 128, 1), side)
-    side_ref[...] = side
-
     lane_f = lax.broadcasted_iota(jnp.int32, (depth, fx), 1)
 
-    for r in range(16):
-        w0[r] = jnp.where(row_ok(r), fp_ref[r], 0.0)
+    for r in range(4, 12):
+        w0[r] = jnp.where(z_ok, fp_ref[r], 0.0)
 
     def advance(field, upper_y, lower_y, behind, c):
         upper_z = pltpu.roll(field, depth - 1, 0)
@@ -358,56 +336,14 @@
     def yaw_term(c, field, value, new):
         return c * (2.0 * FORCE_GAIN * field * value - 3.0 * POWER_GAIN * c * new * new)
 
-    for r in range(1, 15):
+    for r in range(5, 11):
         new = forward(0, w0, r, c0)
         u1[r] = new
         w1[r] = jnp.where(row_ok(r), new, 0.0)
-    for r in range(2, 14):
+    for r in range(6, 10):
         new = forward(1, w1, r, c1)
         u2[r] = new
         lam[r] = power_slope(c1[r], new)
-    for r in range(4, rows + 4):
-        farm_ref[r - 4] = u2[r][0:zd]
-        gc1[r - 4] = yaw_term(c1[r], w1[r], lam[r], u2[r])[0:zd]
-
-    def spread_terms(step, r):
-        value = lam[r]
-        am[r] = value * nu[step, r]
-        bm[r] = value * ry[step, r]
-
-    def backward(step, r, cos_field):
-        value = lam[r]
-        a = am[r]
-        b = value * rz[step, r]
-        c = cos_field[r]
-        ahead = jnp.where(lane_f == fx - 1, 0.0, pltpu.roll(value, fx - 1, 1))
-        total = value * ((1.0 - COURANT) - FORCE_GAIN * (c * c)) + COURANT * ahead - 4.0 * a
-        total = total + (am[r - 1] + bm[r - 1]) + (am[r + 1] - bm[r + 1])
-        return total + pltpu.roll(a + b, 1, 0) + pltpu.roll(a - b, depth - 1, 0)
-
-    for r in range(2, 14):
-        spread_terms(1, r)
-    for r in range(3, 13):
-        value = backward(1, r, c1) + power_slope(c0[r], u1[r])
-        u2[r] = jnp.where(row_ok(r), value, 0.0)
-    for r in range(3, 13):
-        lam[r] = u2[r]
-    for r in range(4, rows + 4):
-        gc0[r - 4] = yaw_term(c0[r], w0[r], lam[r], u1[r])[0:zd]
-    for r in range(3, 13):
-        spread_terms(0, r)
-    for r in range(4, rows + 4):
-        sens_ref[r - 4] = backward(0, r, c0)[0:zd]
-
-    flat = turned[0][:, 0:1] // fx
-    take = (flat == lax.broadcasted_iota(jnp.int32, (count, rows * zd), 1)).astype(F32).astype(BF16)
-    far_along = jnp.where(along[0] >= 18, along[0], -1)
-    for s, terms in ((0, gc0), (1, gc1)):
-        hi, lo = split2(terms[...].reshape(rows * zd, fx))
-        lines = dot(take, lo) + dot(take, hi)
-        value = jnp.where(far_along == lane_x, lines, 0.0)
-        part_ref[s] = value[:, 0:128] + value[:, 128:256]
-
     lax.fori_loop(1, n, far_wait, 0)
 
     base = 4 * odd
@@ -434,13 +370,9 @@
     for last in lasts:
         last.start()
 
-    for i in range(1, planes + 3):
-        v1[i] = periodic_row(vp_ref, i, True)
-    for i in range(2, planes + 2):
-        prec_ref[i - 2] = periodic_row(v1, i, True)[0:zd]
-
     for last in lasts:
         last.wait()
+
 
     for i in range(1, 15):
         vw1[i] = periodic_row(w_ref, i, False)
@@ -491,15 +423,79 @@
     tf0 = yaw_term(cf0, front0, power_slope(cf0, uf1), uf1)
     tf1 = yaw_term(cf1, front1, power_slope(cf1, uf2), uf2)
 
+    @pl.when(g < n - 1)
+    def _():
+        for i in upward:
+            copies[i].wait_send()
+        for i in downward:
+            copies[i].wait_recv()
+
+    @pl.when(g > 0)
+    def _():
+        for i in downward:
+            copies[i].wait_send()
+        for i in upward:
+            copies[i].wait_recv()
+
+    side = jnp.zeros((depth, 128), F32)
+    for r in range(16):
+        side = jnp.where(lane_r == r, pltpu.roll(fp_ref[r, :, 0:128], (8 * r - 14) % 128, 1), side)
+    side_ref[...] = side
+
+    def spread_terms(step, r):
+        value = lam[r]
+        am[r] = value * nu[step, r]
+        bm[r] = value * ry[step, r]
+
+    def backward(step, r, cos_field):
+        value = lam[r]
+        a = am[r]
+        b = value * rz[step, r]
+        c = cos_field[r]
+        ahead = jnp.where(lane_f == fx - 1, 0.0, pltpu.roll(value, fx - 1, 1))
+        total = value * ((1.0 - COURANT) - FORCE_GAIN * (c * c)) + COURANT * ahead - 4.0 * a
+        total = total + (am[r - 1] + bm[r - 1]) + (am[r + 1] - bm[r + 1])
+        return total + pltpu.roll(a + b, 1, 0) + pltpu.roll(a - b, depth - 1, 0)
+
+    for r in (0, 1, 2, 3, 12, 13, 14, 15):
+        w0[r] = jnp.where(row_ok(r), fp_ref[r], 0.0)
+    for r in (1, 2, 3, 4, 11, 12, 13, 14):
+        new = forward(0, w0, r, c0)
+        u1[r] = new
+        w1[r] = jnp.where(row_ok(r), new, 0.0)
+    for r in (2, 3, 4, 5, 10, 11, 12, 13):
+        new = forward(1, w1, r, c1)
+        u2[r] = new
+        lam[r] = power_slope(c1[r], new)
+    for r in range(4, rows + 4):
+        gc1[r - 4] = yaw_term(c1[r], w1[r], lam[r], u2[r])[0:zd]
+        farm_ref[r - 4] = u2[r][0:zd]
+    for r in range(2, 14):
+        spread_terms(1, r)
+    for r in range(3, 13):
+        value = backward(1, r, c1) + power_slope(c0[r], u1[r])
+        u2[r] = jnp.where(row_ok(r), value, 0.0)
+    for r in range(3, 13):
+        lam[r] = u2[r]
+    for r in range(4, rows + 4):
+        gc0[r - 4] = yaw_term(c0[r], w0[r], lam[r], u1[r])[0:zd]
     ws0 = jnp.where(side_ok, jnp.where(lane_k == 1, beside0, side_ref[...]), 0.0)
     us1, *back0 = side_step(ws0, cs0)
     ws1 = jnp.where(side_ok, jnp.where(lane_k == 1, beside1, us1), 0.0)
     us2, *back1 = side_step(ws1, cs1)
     value2 = power_slope(cs1, us2)
     value1 = jnp.where(side_ok, side_back(value2, cs1, *back1) + power_slope(cs0, us1), 0.0)
-    ss = side_back(value1, cs0, *back0)
     ts0 = yaw_term(cs0, ws0, value1, us1)
     ts1 = yaw_term(cs1, ws1, value2, us2)
+
+    flat = turned[0][:, 0:1] // fx
+    take = (flat == lax.broadcasted_iota(jnp.int32, (count, rows * zd), 1)).astype(F32).astype(BF16)
+    far_along = jnp.where(along[0] >= 18, along[0], -1)
+    for s, terms in ((0, gc0), (1, gc1)):
+        hi, lo = split2(terms[...].reshape(rows * zd, fx))
+        lines = dot(take, lo) + dot(take, hi)
+        value = jnp.where(far_along == lane_x, lines, 0.0)
+        part_ref[s] = value[:, 0:128] + value[:, 128:256]
 
     terms = jnp.concatenate([tf0, ts0, tf1, ts1], axis=1)[0:zd]
     hi, lo = split2(terms)
@@ -546,6 +542,13 @@
 
     lax.fori_loop(1, n * m, start(near_copy), 0)
 
+    for r in range(3, 13):
+        spread_terms(0, r)
+    for r in range(4, rows + 4):
+        sens_ref[r - 4] = backward(0, r, c0)[0:zd]
+
+    ss = side_back(value1, cs0, *back0)
+
     us2, ss, uf2 = us2[0:zd], ss[0:zd], uf2[0:zd]
     for r in range(rows):
         shift = (-18 - 8 * r) % 128
@@ -557,6 +560,14 @@
             lane128 < NF, 0.0,
             jnp.where(lane128 < 18, pltpu.roll(ss, shift, 1), sens_ref[r, :, 0:128]),
         )
+
+    for i in range(5, 10):
+        copies[i].wait()
+
+    for i in range(1, planes + 3):
+        v1[i] = periodic_row(vp_ref, i, True)
+    for i in range(2, planes + 2):
+        prec_ref[i - 2] = periodic_row(v1, i, True)[0:zd]
 
     lax.fori_loop(1, n * m, wait(near_copy), 0)
     total_b[scen] = jnp.sum(total_a[...], axis=0)

time: 37.2 us -> 34.6 us (0.930)
  Pallas kernels: 36.4 us -> 33.8 us
    pallas_call x1, Pallas kernels: 35.3 us -> 32.7 us  [farm_steps(): pl.pallas_call(functools.partial(farm_kernel, sizes), out_shape=(pltpu.VM...]
where the time goes in v3:
time: 34.6 us; the launch traced here: 34.4 us
  Pallas kernels  33.8 us (98%)
  between operations  0.64 us (2%)
    pallas_call x1, Pallas kernels, farm_steps(): pl.pallas_call(functools.partial(farm_kernel, sizes), out_shape=(pltpu.VM...  32.7 us
    pallas_call x1, Pallas kernels, finish(): pl.pallas_call(finish_kernel, out_shape=tuple((jax.ShapeDtypeStruct(x.sha...  1.09 us

profile of v3, /device:TPU:0, one launch (start us, length us, event | category | flops | bytes accessed | tf_op | source)
XLA Modules:
  0.0 34.4 jit_solution(7728864922780901094)
XLA Ops:
  0.6 32.7 %farm_steps.1 = (f32[8,64,128]{2,1,0:T(8,128)S(1)}, f32[8,64,256]{2,1,0:T(8,128)S(1)}, f32[8,64,256]{2,1,0:T(8,128)S(1)}, f32[2,64]{1,0:T(2,128)S(1)}) custom-call(f32[8,64,128]{2,1,0:T(8,128)} %bitcast.8, f32[8,64,256]{2,1,0:T(8,128)} %bitcast.7, s32[1,128]{1,0:T(1,128)} %bitcast.9, s32[1,128]{1,0:T(1,128)} %bitcast.10, f32[2,64]{1,0:T(2,128)} %yaw_in.1, ...), custom_call_target="tpu_custom_call" | custom-call | tf_op jit(solution)/shard_map/farm_steps/pallas_call | solution.py:587
  33.3 1.1 %finish.1 = (f32[8,64,128]{2,1,0:T(8,128)}, f32[8,64,256]{2,1,0:T(8,128)}, f32[8,64,256]{2,1,0:T(8,128)}, f32[2,64]{1,0:T(2,128)}) custom-call(f32[8,64,128]{2,1,0:T(8,128)S(1)} %get-tuple-element.12.refs_0_, f32[8,64,256]{2,1,0:T(8,128)S(1)} %get-tuple-element.13.refs_1_, f32[8,64,256]{2,1,0:T(8,128)S(1)} %get-tuple-element.14.refs_2_, ...), custom_call_target="tpu_custom_call" | custom-call | tf_op jit(solution)/shard_map/finish/pallas_call | solution.py:651

commit v4 on v2

--- a/solution.py
+++ b/solution.py
@@ -62,10 +62,10 @@
     prec_ref, farm_ref, sens_ref, grad_ref,
     fp_ref, vp_ref, w_ref, cb_ref,
     v_ref, u_ref, cell_ref, index_ref, turbine_ref, yaw_ref, in_sem,
-    vedge, uedge, bsend, rbody, wedge,
+    vedge, uedge, bsend, rbody, esend, ebody,
     v1, vw1, vw2, c0, c1, w0, w1, u1, u2, lam, nu, ry, rz, am, bm, gc0, gc1, total_a, total_b,
     pick_ref, cp_ref, side_ref, part_ref,
-    near_send, near_recv, far_send, far_recv, edge_send, edge_recv, a_send, a_recv, b_send, b_recv,
+    near_send, near_recv, far_send, far_recv, rim_send, rim_recv, edge_send, edge_recv, a_send, a_recv, b_send, b_recv,
 ):
     g = lax.axis_index("grp")
     p = lax.axis_index("pen")
@@ -174,13 +174,11 @@
         for i, (src, dst, tg, tp) in enumerate(moves)
     ]
     upward, downward, aside = (0, 3), (1, 4), (2,)
+    copies[7].start()
     for i in range(10, 15):
-        copies[i].start()
-    for i in range(5, 10):
         copies[i].start()
     for i in aside:
         copies[i].start()
-
     @pl.when(g < n - 1)
     def _():
         for i in upward:
@@ -191,8 +189,39 @@
         for i in downward:
             copies[i].start()
 
-    lax.fori_loop(1, n, far_start, 0)
-
+    lax.fori_loop(n // 2 - 2, n // 2 + 3, far_start, 0)
+
+    def rim_copy(d):
+        target = lax.rem(g + d, n)
+        return pltpu.make_async_remote_copy(
+            src_ref=esend.at[target], dst_ref=ebody.at[pl.ds(g * planes, planes)],
+            send_sem=rim_send.at[d], recv_sem=rim_recv.at[d],
+            device_id={"grp": target, "pen": p}, device_id_type=MESH,
+        )
+
+    def rim_start(d, carry):
+        rim_copy(d).start()
+        return carry
+
+    def rim_wait(d, carry):
+        rim_copy(d).wait()
+        return carry
+
+    copies[7].wait()
+    for x in range(planes):
+        edge = vp_ref[x + 2, zd : zd + 8]
+        tall = jnp.concatenate(
+            [edge if i == 4 else pltpu.roll(edge, (4 - i) % fy, 1) for i in range(16)], axis=0
+        ).T
+        esend[:, x, :] = tall.reshape(n, rows, 128)[:, 0]
+    lax.fori_loop(1, n, rim_start, 0)
+    lax.fori_loop(n // 2 + 3, n, far_start, 0)
+    lax.fori_loop(1, n // 2 - 2, far_start, 0)
+
+    for i in (5, 6, 8, 9):
+        copies[i].start()
+
+    ebody[pl.ds(g * planes, planes)] = esend[g]
     fp_ref[4 : rows + 4, 0:zd] = u_ref[...]
     vp_ref[2 : planes + 2, 0:zd] = v_ref[...]
     cb_ref[0] = cell_ref[...]
@@ -301,35 +330,13 @@
         far(d).wait()
         return carry
 
-    for i in range(5, 10):
-        copies[i].wait()
-
     for i in aside:
         copies[i].wait()
 
-    @pl.when(g < n - 1)
-    def _():
-        for i in upward:
-            copies[i].wait_send()
-        for i in downward:
-            copies[i].wait_recv()
-
-    @pl.when(g > 0)
-    def _():
-        for i in downward:
-            copies[i].wait_send()
-        for i in upward:
-            copies[i].wait_recv()
-
-    side = jnp.zeros((depth, 128), F32)
-    for r in range(16):
-        side = jnp.where(lane_r == r, pltpu.roll(fp_ref[r, :, 0:128], (8 * r - 14) % 128, 1), side)
-    side_ref[...] = side
-
     lane_f = lax.broadcasted_iota(jnp.int32, (depth, fx), 1)
 
-    for r in range(16):
-        w0[r] = jnp.where(row_ok(r), fp_ref[r], 0.0)
+    for r in range(4, 12):
+        w0[r] = jnp.where(z_ok, fp_ref[r], 0.0)
 
     def advance(field, upper_y, lower_y, behind, c):
         upper_z = pltpu.roll(field, depth - 1, 0)
@@ -358,17 +365,32 @@
     def yaw_term(c, field, value, new):
         return c * (2.0 * FORCE_GAIN * field * value - 3.0 * POWER_GAIN * c * new * new)
 
-    for r in range(1, 15):
+    for r in range(5, 11):
         new = forward(0, w0, r, c0)
         u1[r] = new
         w1[r] = jnp.where(row_ok(r), new, 0.0)
-    for r in range(2, 14):
+    for r in range(6, 10):
         new = forward(1, w1, r, c1)
         u2[r] = new
         lam[r] = power_slope(c1[r], new)
-    for r in range(4, rows + 4):
-        farm_ref[r - 4] = u2[r][0:zd]
-        gc1[r - 4] = yaw_term(c1[r], w1[r], lam[r], u2[r])[0:zd]
+    @pl.when(g < n - 1)
+    def _():
+        for i in upward:
+            copies[i].wait_send()
+        for i in downward:
+            copies[i].wait_recv()
+
+    @pl.when(g > 0)
+    def _():
+        for i in downward:
+            copies[i].wait_send()
+        for i in upward:
+            copies[i].wait_recv()
+
+    side = jnp.zeros((depth, 128), F32)
+    for r in range(16):
+        side = jnp.where(lane_r == r, pltpu.roll(fp_ref[r, :, 0:128], (8 * r - 14) % 128, 1), side)
+    side_ref[...] = side
 
     def spread_terms(step, r):
         value = lam[r]
@@ -385,6 +407,19 @@
         total = total + (am[r - 1] + bm[r - 1]) + (am[r + 1] - bm[r + 1])
         return total + pltpu.roll(a + b, 1, 0) + pltpu.roll(a - b, depth - 1, 0)
 
+    for r in (0, 1, 2, 3, 12, 13, 14, 15):
+        w0[r] = jnp.where(row_ok(r), fp_ref[r], 0.0)
+    for r in (1, 2, 3, 4, 11, 12, 13, 14):
+        new = forward(0, w0, r, c0)
+        u1[r] = new
+        w1[r] = jnp.where(row_ok(r), new, 0.0)
+    for r in (2, 3, 4, 5, 10, 11, 12, 13):
+        new = forward(1, w1, r, c1)
+        u2[r] = new
+        lam[r] = power_slope(c1[r], new)
+    for r in range(4, rows + 4):
+        gc1[r - 4] = yaw_term(c1[r], w1[r], lam[r], u2[r])[0:zd]
+        farm_ref[r - 4] = u2[r][0:zd]
     for r in range(2, 14):
         spread_terms(1, r)
     for r in range(3, 13):
@@ -394,11 +429,6 @@
         lam[r] = u2[r]
     for r in range(4, rows + 4):
         gc0[r - 4] = yaw_term(c0[r], w0[r], lam[r], u1[r])[0:zd]
-    for r in range(3, 13):
-        spread_terms(0, r)
-    for r in range(4, rows + 4):
-        sens_ref[r - 4] = backward(0, r, c0)[0:zd]
-
     flat = turned[0][:, 0:1] // fx
     take = (flat == lax.broadcasted_iota(jnp.int32, (count, rows * zd), 1)).astype(F32).astype(BF16)
     far_along = jnp.where(along[0] >= 18, along[0], -1)
@@ -410,41 +440,40 @@
 
     lax.fori_loop(1, n, far_wait, 0)
 
-    base = 4 * odd
+    lax.fori_loop(1, n, rim_wait, 0)
+
     for i in range(6):
         flipped = rbody[i].T
         for h in range(2):
-            part = flipped[h * zd : (h + 1) * zd]
-            w_ref[base + h * 6 + i, 0:zd] = part
-            wedge[base + h * 6 + i, 0:4] = part[0:4]
-            wedge[base + h * 6 + i, 4:8] = part[zd - 4 : zd]
-    inner, outer = 8 - base, 12 * odd
+            k = h * 6 + i
+            w_ref[k + odd * (11 - 2 * k), 0:zd] = flipped[h * zd : (h + 1) * zd]
     mated = g + 1 - 2 * odd
     lasts = [
         pltpu.make_async_remote_copy(
-            src_ref=src, dst_ref=dst, send_sem=edge_send.at[i], recv_sem=edge_recv.at[i],
-            device_id={"grp": target, "pen": side_pen}, device_id_type=MESH,
-        )
-        for i, (src, dst, target, side_pen) in enumerate((
-            (wedge.at[pl.ds(base, 12)], w_ref.at[pl.ds(base, 12), zd : zd + 8], g, q),
-            (wedge.at[pl.ds(inner, 4)], w_ref.at[pl.ds(outer, 4), zd : zd + 8], mated, q),
-            (w_ref.at[pl.ds(inner, 4), 0:zd], w_ref.at[pl.ds(outer, 4), 0:zd], mated, p),
-        ))
+            src_ref=w_ref.at[8 + k, 0:zd], dst_ref=w_ref.at[15 - k, 0:zd],
+            send_sem=edge_send.at[k], recv_sem=edge_recv.at[k],
+            device_id={"grp": mated, "pen": p}, device_id_type=MESH,
+        )
+        for k in range(4)
     ]
     for last in lasts:
         last.start()
-
-    for i in range(1, planes + 3):
-        v1[i] = periodic_row(vp_ref, i, True)
-    for i in range(2, planes + 2):
-        prec_ref[i - 2] = periodic_row(v1, i, True)[0:zd]
+    rims = ebody[...].T
+    for r in range(16):
+        w_ref[r + odd * (15 - 2 * r), zd : zd + 8] = rims[8 * r : 8 * r + 8]
+
+    for i in range(1, 11):
+        vw1[i] = periodic_row(w_ref, i, False)
+    for i in range(2, 10):
+        vw2[i] = periodic_row(vw1, i, False)
 
     for last in lasts:
         last.wait()
 
-    for i in range(1, 15):
+
+    for i in range(11, 15):
         vw1[i] = periodic_row(w_ref, i, False)
-    for i in range(2, 14):
+    for i in range(10, 14):
         vw2[i] = periodic_row(vw1, i, False)
 
     def inlets(src, first, stop):
@@ -455,13 +484,14 @@
         beside = front
         for r in range(first, stop):
             part = found[(r - first) * depth : (r - first + 1) * depth]
+            row = r + odd * (15 - 2 * r)
             if 4 <= r < 12:
-                front = jnp.where(lane128 // NF == r - 4, part[:, 0:128], front)
+                front = jnp.where(lane128 // NF == row - 4, part[:, 0:128], front)
             elif r == 3:
-                rim = jnp.where(lane128 < 64, part[:, 0:128], rim)
+                rim = jnp.where(lane128 // 64 == odd, part[:, 0:128], rim)
             elif r == 12:
-                rim = jnp.where(lane128 >= 64, part[:, 0:128], rim)
-            beside = jnp.where(lane_r == r, part[:, 128:256], beside)
+                rim = jnp.where(lane128 // 64 == 1 - odd, part[:, 0:128], rim)
+            beside = jnp.where(lane_r == row, part[:, 128:256], beside)
         return jnp.where(z_ok, front, 0.0), jnp.where(edge_ok, rim, 0.0), beside
 
     def front_step(field, rim, c):
@@ -497,7 +527,6 @@
     us2, *back1 = side_step(ws1, cs1)
     value2 = power_slope(cs1, us2)
     value1 = jnp.where(side_ok, side_back(value2, cs1, *back1) + power_slope(cs0, us1), 0.0)
-    ss = side_back(value1, cs0, *back0)
     ts0 = yaw_term(cs0, ws0, value1, us1)
     ts1 = yaw_term(cs1, ws1, value2, us2)
 
@@ -546,6 +575,13 @@
 
     lax.fori_loop(1, n * m, start(near_copy), 0)
 
+    for r in range(3, 13):
+        spread_terms(0, r)
+    for r in range(4, rows + 4):
+        sens_ref[r - 4] = backward(0, r, c0)[0:zd]
+
+    ss = side_back(value1, cs0, *back0)
+
     us2, ss, uf2 = us2[0:zd], ss[0:zd], uf2[0:zd]
     for r in range(rows):
         shift = (-18 - 8 * r) % 128
@@ -557,6 +593,14 @@
             lane128 < NF, 0.0,
             jnp.where(lane128 < 18, pltpu.roll(ss, shift, 1), sens_ref[r, :, 0:128]),
         )
+
+    for i in (5, 6, 8, 9):
+        copies[i].wait()
+
+    for i in range(1, planes + 3):
+        v1[i] = periodic_row(vp_ref, i, True)
+    for i in range(2, planes + 2):
+        prec_ref[i - 2] = periodic_row(v1, i, True)[0:zd]
 
     lax.fori_loop(1, n * m, wait(near_copy), 0)
     total_b[scen] = jnp.sum(total_a[...], axis=0)
@@ -599,7 +643,8 @@
             pltpu.VMEM((rows, 8, fx), F32),
             pltpu.VMEM((fy + 8, planes, 2 * zd), F32),
             pltpu.VMEM((6, px, 2 * zd), F32),
-            pltpu.VMEM((16, 8, px), F32),
+            pltpu.VMEM((n, planes, 128), F32),
+            pltpu.VMEM((px, 128), F32),
             pltpu.VMEM((planes + 4, depth, fy), F32),
             pltpu.VMEM((16, depth, px), F32),
             pltpu.VMEM((16, depth, px), F32),
@@ -616,7 +661,7 @@
             pltpu.VMEM((4, depth, 128), F32),
             pltpu.VMEM((depth, 128), F32),
             pltpu.VMEM((2, index.shape[1], 128), F32),
-            dma((15,)), dma((15,)), dma((n,)), dma((n,)), dma((3,)), dma((3,)),
+            dma((15,)), dma((15,)), dma((n,)), dma((n,)), dma((n,)), dma((n,)), dma((4,)), dma((4,)),
             dma((n * m,)), dma((n * m,)), dma((ns,)), dma((ns,)),
         ],
         compiler_params=pltpu.CompilerParams(

time: 37.2 us -> 33 us (0.89)
  Pallas kernels: 36.4 us -> 32.2 us
    pallas_call x1, Pallas kernels: 35.3 us -> 31.1 us  [farm_steps(): pl.pallas_call(functools.partial(farm_kernel, sizes), out_shape=(pltpu.VM...]
where the time goes in v4:
time: 33 us; the launch traced here: 32.8 us
  Pallas kernels  32.2 us (98%)
  between operations  0.64 us (2%)
    pallas_call x1, Pallas kernels, farm_steps(): pl.pallas_call(functools.partial(farm_kernel, sizes), out_shape=(pltpu.VM...  31.1 us
    pallas_call x1, Pallas kernels, finish(): pl.pallas_call(finish_kernel, out_shape=tuple((jax.ShapeDtypeStruct(x.sha...  1.09 us

profile of v4, /device:TPU:0, one launch (start us, length us, event | category | flops | bytes accessed | tf_op | source)
XLA Modules:
  0.0 32.8 jit_solution(18150869432117982160)
XLA Ops:
  0.6 31.1 %farm_steps.1 = (f32[8,64,128]{2,1,0:T(8,128)S(1)}, f32[8,64,256]{2,1,0:T(8,128)S(1)}, f32[8,64,256]{2,1,0:T(8,128)S(1)}, f32[2,64]{1,0:T(2,128)S(1)}) custom-call(f32[8,64,128]{2,1,0:T(8,128)} %bitcast.8, f32[8,64,256]{2,1,0:T(8,128)} %bitcast.7, s32[1,128]{1,0:T(1,128)} %bitcast.9, s32[1,128]{1,0:T(1,128)} %bitcast.10, f32[2,64]{1,0:T(2,128)} %yaw_in.1, ...), custom_call_target="tpu_custom_call" | custom-call | tf_op jit(solution)/shard_map/farm_steps/pallas_call | solution.py:620
  31.8 1.1 %finish.1 = (f32[8,64,128]{2,1,0:T(8,128)}, f32[8,64,256]{2,1,0:T(8,128)}, f32[8,64,256]{2,1,0:T(8,128)}, f32[2,64]{1,0:T(2,128)}) custom-call(f32[8,64,128]{2,1,0:T(8,128)S(1)} %get-tuple-element.12.refs_0_, f32[8,64,256]{2,1,0:T(8,128)S(1)} %get-tuple-element.13.refs_1_, f32[8,64,256]{2,1,0:T(8,128)S(1)} %get-tuple-element.14.refs_2_, ...), custom_call_target="tpu_custom_call" | custom-call | tf_op jit(solution)/shard_map/finish/pallas_call | solution.py:685

commit v5 on v4

--- a/solution.py
+++ b/solution.py
@@ -189,7 +189,7 @@
         for i in downward:
             copies[i].start()
 
-    lax.fori_loop(n // 2 - 2, n // 2 + 3, far_start, 0)
+    lax.fori_loop(n // 4, n - n // 4 + 1, far_start, 0)
 
     def rim_copy(d):
         target = lax.rem(g + d, n)
@@ -215,11 +215,8 @@
         ).T
         esend[:, x, :] = tall.reshape(n, rows, 128)[:, 0]
     lax.fori_loop(1, n, rim_start, 0)
-    lax.fori_loop(n // 2 + 3, n, far_start, 0)
-    lax.fori_loop(1, n // 2 - 2, far_start, 0)
-
-    for i in (5, 6, 8, 9):
-        copies[i].start()
+    lax.fori_loop(n - n // 4 + 1, n, far_start, 0)
+    lax.fori_loop(1, n // 4, far_start, 0)
 
     ebody[pl.ds(g * planes, planes)] = esend[g]
     fp_ref[4 : rows + 4, 0:zd] = u_ref[...]
@@ -458,6 +455,9 @@
     ]
     for last in lasts:
         last.start()
+    for i in (5, 6, 8, 9):
+        copies[i].start()
+
     rims = ebody[...].T
     for r in range(16):
         w_ref[r + odd * (15 - 2 * r), zd : zd + 8] = rims[8 * r : 8 * r + 8]

time: 33 us -> 32.2 us (0.976)
  Pallas kernels: 32.2 us -> 31.4 us
    pallas_call x1, Pallas kernels: 31.1 us -> 30.3 us  [farm_steps(): pl.pallas_call(functools.partial(farm_kernel, sizes), out_shape=(pltpu.VM...]
where the time goes in v5:
time: 32.2 us; the launch traced here: 32.1 us
  Pallas kernels  31.4 us (98%)
  between operations  0.64 us (2%)
    pallas_call x1, Pallas kernels, farm_steps(): pl.pallas_call(functools.partial(farm_kernel, sizes), out_shape=(pltpu.VM...  30.3 us
    pallas_call x1, Pallas kernels, finish(): pl.pallas_call(finish_kernel, out_shape=tuple((jax.ShapeDtypeStruct(x.sha...  1.09 us

profile of v5, /device:TPU:0, one launch (start us, length us, event | category | flops | bytes accessed | tf_op | source)
XLA Modules:
  0.0 32.1 jit_solution(14119432430969056749)
XLA Ops:
  0.6 30.3 %farm_steps.1 = (f32[8,64,128]{2,1,0:T(8,128)S(1)}, f32[8,64,256]{2,1,0:T(8,128)S(1)}, f32[8,64,256]{2,1,0:T(8,128)S(1)}, f32[2,64]{1,0:T(2,128)S(1)}) custom-call(f32[8,64,128]{2,1,0:T(8,128)} %bitcast.8, f32[8,64,256]{2,1,0:T(8,128)} %bitcast.7, s32[1,128]{1,0:T(1,128)} %bitcast.9, s32[1,128]{1,0:T(1,128)} %bitcast.10, f32[2,64]{1,0:T(2,128)} %yaw_in.1, ...), custom_call_target="tpu_custom_call" | custom-call | tf_op jit(solution)/shard_map/farm_steps/pallas_call | solution.py:620
  31.0 1.1 %finish.1 = (f32[8,64,128]{2,1,0:T(8,128)}, f32[8,64,256]{2,1,0:T(8,128)}, f32[8,64,256]{2,1,0:T(8,128)}, f32[2,64]{1,0:T(2,128)}) custom-call(f32[8,64,128]{2,1,0:T(8,128)S(1)} %get-tuple-element.12.refs_0_, f32[8,64,256]{2,1,0:T(8,128)S(1)} %get-tuple-element.13.refs_1_, f32[8,64,256]{2,1,0:T(8,128)S(1)} %get-tuple-element.14.refs_2_, ...), custom_call_target="tpu_custom_call" | custom-call | tf_op jit(solution)/shard_map/finish/pallas_call | solution.py:685

commit v6 on v5

--- a/solution.py
+++ b/solution.py
@@ -138,8 +138,8 @@
         return pltpu.make_async_remote_copy(
             src_ref=bsend.at[pl.ds(target * 8 + 4 * lax.rem(target, 2), 6)],
             dst_ref=rbody.at[:, pl.ds(g * planes, planes)],
-            send_sem=far_send.at[d],
-            recv_sem=far_recv.at[d],
+            send_sem=far_send,
+            recv_sem=far_recv,
             device_id={"grp": target, "pen": p},
             device_id_type=MESH,
         )
@@ -195,7 +195,7 @@
         target = lax.rem(g + d, n)
         return pltpu.make_async_remote_copy(
             src_ref=esend.at[target], dst_ref=ebody.at[pl.ds(g * planes, planes)],
-            send_sem=rim_send.at[d], recv_sem=rim_recv.at[d],
+            send_sem=rim_send, recv_sem=rim_recv,
             device_id={"grp": target, "pen": p}, device_id_type=MESH,
         )
 
@@ -203,9 +203,11 @@
         rim_copy(d).start()
         return carry
 
-    def rim_wait(d, carry):
-        rim_copy(d).wait()
-        return carry
+    def bulk_wait(landed, send_sem, recv_sem):
+        pltpu.make_async_remote_copy(
+            src_ref=landed, dst_ref=landed, send_sem=send_sem, recv_sem=recv_sem,
+            device_id={"grp": up, "pen": p}, device_id_type=MESH,
+        ).wait()
 
     copies[7].wait()
     for x in range(planes):
@@ -322,10 +324,6 @@
     for k in range(4):
         part = packed[:, k * 128 : (k + 1) * 128]
         cp_ref[k] = jnp.where(side_ok if k % 2 else z_ok, part, 0.0)
-
-    def far_wait(d, carry):
-        far(d).wait()
-        return carry
 
     for i in aside:
         copies[i].wait()
@@ -435,9 +433,9 @@
         value = jnp.where(far_along == lane_x, lines, 0.0)
         part_ref[s] = value[:, 0:128] + value[:, 128:256]
 
-    lax.fori_loop(1, n, far_wait, 0)
-
-    lax.fori_loop(1, n, rim_wait, 0)
+    bulk_wait(rbody.at[:, 0 : px - planes], far_send, far_recv)
+
+    bulk_wait(ebody.at[0 : px - planes], rim_send, rim_recv)
 
     for i in range(6):
         flipped = rbody[i].T
@@ -550,7 +548,7 @@
     def near_copy(d):
         return pltpu.make_async_remote_copy(
             src_ref=total_a.at[g * m + p], dst_ref=total_a.at[g * m + p],
-            send_sem=a_send.at[d], recv_sem=a_recv.at[d], device_id=peer(d), device_id_type=MESH,
+            send_sem=a_send, recv_sem=a_recv, device_id=peer(d), device_id_type=MESH,
         )
 
     def line_copy(d):
@@ -602,7 +600,7 @@
     for i in range(2, planes + 2):
         prec_ref[i - 2] = periodic_row(v1, i, True)[0:zd]
 
-    lax.fori_loop(1, n * m, wait(near_copy), 0)
+    bulk_wait(total_a.at[0 : n * m - 1], a_send, a_recv)
     total_b[scen] = jnp.sum(total_a[...], axis=0)
     lax.fori_loop(1, ns, start(line_copy), 0)
     lax.fori_loop(1, ns, wait(line_copy), 0)
@@ -661,8 +659,8 @@
             pltpu.VMEM((4, depth, 128), F32),
             pltpu.VMEM((depth, 128), F32),
             pltpu.VMEM((2, index.shape[1], 128), F32),
-            dma((15,)), dma((15,)), dma((n,)), dma((n,)), dma((n,)), dma((n,)), dma((4,)), dma((4,)),
-            dma((n * m,)), dma((n * m,)), dma((ns,)), dma((ns,)),
+            dma((15,)), dma((15,)), dma, dma, dma, dma, dma((4,)), dma((4,)),
+            dma, dma, dma((ns,)), dma((ns,)),
         ],
         compiler_params=pltpu.CompilerParams(
             collective_id=0, has_side_effects=True, vmem_limit_bytes=56 * 1024 * 1024

time: 32.2 us -> 30.9 us (0.960)
  Pallas kernels: 31.4 us -> 30.1 us
    pallas_call x1, Pallas kernels: 30.3 us -> 29 us  [farm_steps(): pl.pallas_call(functools.partial(farm_kernel, sizes), out_shape=(pltpu.VM...]
where the time goes in v6:
time: 30.9 us; the launch traced here: 30.8 us
  Pallas kernels  30.1 us (97%)
  between operations  0.64 us (2%)
    pallas_call x1, Pallas kernels, farm_steps(): pl.pallas_call(functools.partial(farm_kernel, sizes), out_shape=(pltpu.VM...  29 us
    pallas_call x1, Pallas kernels, finish(): pl.pallas_call(finish_kernel, out_shape=tuple((jax.ShapeDtypeStruct(x.sha...  1.09 us

profile of v6, /device:TPU:0, one launch (start us, length us, event | category | flops | bytes accessed | tf_op | source)
XLA Modules:
  0.0 30.8 jit_solution(18245504363140342990)
XLA Ops:
  0.6 29.0 %farm_steps.1 = (f32[8,64,128]{2,1,0:T(8,128)S(1)}, f32[8,64,256]{2,1,0:T(8,128)S(1)}, f32[8,64,256]{2,1,0:T(8,128)S(1)}, f32[2,64]{1,0:T(2,128)S(1)}) custom-call(f32[8,64,128]{2,1,0:T(8,128)} %bitcast.8, f32[8,64,256]{2,1,0:T(8,128)} %bitcast.7, s32[1,128]{1,0:T(1,128)} %bitcast.9, s32[1,128]{1,0:T(1,128)} %bitcast.10, f32[2,64]{1,0:T(2,128)} %yaw_in.1, ...), custom_call_target="tpu_custom_call" | custom-call | tf_op jit(solution)/shard_map/farm_steps/pallas_call | solution.py:618
  29.7 1.1 %finish.1 = (f32[8,64,128]{2,1,0:T(8,128)}, f32[8,64,256]{2,1,0:T(8,128)}, f32[8,64,256]{2,1,0:T(8,128)}, f32[2,64]{1,0:T(2,128)}) custom-call(f32[8,64,128]{2,1,0:T(8,128)S(1)} %get-tuple-element.12.refs_0_, f32[8,64,256]{2,1,0:T(8,128)S(1)} %get-tuple-element.13.refs_1_, f32[8,64,256]{2,1,0:T(8,128)S(1)} %get-tuple-element.14.refs_2_, ...), custom_call_target="tpu_custom_call" | custom-call | tf_op jit(solution)/shard_map/finish/pallas_call | solution.py:683

commit v7 on v6

--- a/solution.py
+++ b/solution.py
@@ -203,11 +203,15 @@
         rim_copy(d).start()
         return carry
 
-    def bulk_wait(landed, send_sem, recv_sem):
-        pltpu.make_async_remote_copy(
+    def bulk(landed, send_sem, recv_sem):
+        return pltpu.make_async_remote_copy(
             src_ref=landed, dst_ref=landed, send_sem=send_sem, recv_sem=recv_sem,
             device_id={"grp": up, "pen": p}, device_id_type=MESH,
-        ).wait()
+        )
+
+    whole_far = bulk(rbody.at[:, 0 : px - planes], far_send, far_recv)
+    whole_rim = bulk(ebody.at[0 : px - planes], rim_send, rim_recv)
+    whole_sum = bulk(total_a.at[0 : n * m - 1], a_send, a_recv)
 
     copies[7].wait()
     for x in range(planes):
@@ -433,9 +437,9 @@
         value = jnp.where(far_along == lane_x, lines, 0.0)
         part_ref[s] = value[:, 0:128] + value[:, 128:256]
 
-    bulk_wait(rbody.at[:, 0 : px - planes], far_send, far_recv)
-
-    bulk_wait(ebody.at[0 : px - planes], rim_send, rim_recv)
+    whole_far.wait_recv()
+
+    whole_rim.wait_recv()
 
     for i in range(6):
         flipped = rbody[i].T
@@ -446,7 +450,7 @@
     lasts = [
         pltpu.make_async_remote_copy(
             src_ref=w_ref.at[8 + k, 0:zd], dst_ref=w_ref.at[15 - k, 0:zd],
-            send_sem=edge_send.at[k], recv_sem=edge_recv.at[k],
+            send_sem=edge_send, recv_sem=edge_recv,
             device_id={"grp": mated, "pen": p}, device_id_type=MESH,
         )
         for k in range(4)
@@ -465,8 +469,7 @@
     for i in range(2, 10):
         vw2[i] = periodic_row(vw1, i, False)
 
-    for last in lasts:
-        last.wait()
+    bulk(w_ref.at[8:12, 0:zd], edge_send, edge_recv).wait()
 
 
     for i in range(11, 15):
@@ -600,7 +603,9 @@
     for i in range(2, planes + 2):
         prec_ref[i - 2] = periodic_row(v1, i, True)[0:zd]
 
-    bulk_wait(total_a.at[0 : n * m - 1], a_send, a_recv)
+    whole_far.wait_send()
+    whole_rim.wait_send()
+    whole_sum.wait()
     total_b[scen] = jnp.sum(total_a[...], axis=0)
     lax.fori_loop(1, ns, start(line_copy), 0)
     lax.fori_loop(1, ns, wait(line_copy), 0)
@@ -659,7 +664,7 @@
             pltpu.VMEM((4, depth, 128), F32),
             pltpu.VMEM((depth, 128), F32),
             pltpu.VMEM((2, index.shape[1], 128), F32),
-            dma((15,)), dma((15,)), dma, dma, dma, dma, dma((4,)), dma((4,)),
+            dma((15,)), dma((15,)), dma, dma, dma, dma, dma, dma,
             dma, dma, dma((ns,)), dma((ns,)),
         ],
         compiler_params=pltpu.CompilerParams(

time: 30.9 us -> 30.9 us (level)
  no operation moved by 1% of the time
where the time goes in v7:
time: 30.9 us; the launch traced here: 30.7 us
  Pallas kernels  30.1 us (97%)
  between operations  0.64 us (2%)
    pallas_call x1, Pallas kernels, farm_steps(): pl.pallas_call(functools.partial(farm_kernel, sizes), out_shape=(pltpu.VM...  29 us
    pallas_call x1, Pallas kernels, finish(): pl.pallas_call(finish_kernel, out_shape=tuple((jax.ShapeDtypeStruct(x.sha...  1.09 us

profile of v7, /device:TPU:0, one launch (start us, length us, event | category | flops | bytes accessed | tf_op | source)
XLA Modules:
  0.0 30.7 jit_solution(2617608500837573514)
XLA Ops:
  0.6 29.0 %farm_steps.1 = (f32[8,64,128]{2,1,0:T(8,128)S(1)}, f32[8,64,256]{2,1,0:T(8,128)S(1)}, f32[8,64,256]{2,1,0:T(8,128)S(1)}, f32[2,64]{1,0:T(2,128)S(1)}) custom-call(f32[8,64,128]{2,1,0:T(8,128)} %bitcast.8, f32[8,64,256]{2,1,0:T(8,128)} %bitcast.7, s32[1,128]{1,0:T(1,128)} %bitcast.9, s32[1,128]{1,0:T(1,128)} %bitcast.10, f32[2,64]{1,0:T(2,128)} %yaw_in.1, ...), custom_call_target="tpu_custom_call" | custom-call | tf_op jit(solution)/shard_map/farm_steps/pallas_call | solution.py:623
  29.6 1.1 %finish.1 = (f32[8,64,128]{2,1,0:T(8,128)}, f32[8,64,256]{2,1,0:T(8,128)}, f32[8,64,256]{2,1,0:T(8,128)}, f32[2,64]{1,0:T(2,128)}) custom-call(f32[8,64,128]{2,1,0:T(8,128)S(1)} %get-tuple-element.12.refs_0_, f32[8,64,256]{2,1,0:T(8,128)S(1)} %get-tuple-element.13.refs_1_, f32[8,64,256]{2,1,0:T(8,128)S(1)} %get-tuple-element.14.refs_2_, ...), custom_call_target="tpu_custom_call" | custom-call | tf_op jit(solution)/shard_map/finish/pallas_call | solution.py:688
